TPU v7x, 32 devices: a whole 2x2x4 slice. The times are simulated.
32 devices in a mesh: parts: 2 (over y), blk: 4 (over z), rows: 4 (over x, core).
Axes of the slice: x: 2, y: 2, z: 4, core: 2. Of those that a mesh axis runs over, the one named last changes fastest.
Arguments:
- tiles: float32 [16, 1024, 1024], P(('parts', 'blk'), 'rows'), parts along dimension 0, may hold values from -6 to 6
- pairs: int32 [8, 2, 2], P(('parts', 'blk')), parts along dimension 0, may hold values from 0 to 3, as said below
- counts: int32 [8], P(('parts', 'blk')), parts along dimension 0, may hold values from 1 to 2, as said below
Outputs:
- surfaces: float32 [16, 1024, 1024], P(('parts', 'blk'), 'rows'), parts along dimension 0
There are 2 independent parts, one for each index of `parts`. A program takes and returns all parts, laid end to end along the dimension named above; each array names one. Nothing has to cross between parts.
Inputs may be any that keep to these rules, and one draw needn't show every extreme that they name: pairs[b, k] = (a, c) with a < 2; c below 2 names a tile of group b, otherwise a tile of the group half the groups away; slot 0 of every group names a tile of that other group. Slots k < counts[b] of group b are live; some group has all 2 slots live.
All inputs are finite; a program needn't handle non-finite values.
Results may differ from a plain program's by a relative error of at most 0.011.
Values may be sent and summed in bfloat16 or wider, within the bound.
A program may use at most 64 MiB of HBM per device.

v0:
```python
import math

import jax
import jax.numpy as jnp
from jax import lax
from jax.sharding import PartitionSpec as P

FLOOR = 0.05


def passed_along(value, axis, steps):
    count = lax.axis_size(axis)
    pairs = [(source, (source + steps) % count) for source in range(count)]
    return lax.ppermute(value, axis, pairs)


def dft_tables(length):
    index = jnp.arange(length, dtype=jnp.int32)
    phase = index[:, None] * index[None, :] % length
    angle = 2.0 * math.pi / length * phase.astype(jnp.float32)
    factor = 1.0 / math.sqrt(length)
    return (
        (jnp.cos(angle) * factor).astype(jnp.bfloat16),
        (jnp.sin(angle) * factor).astype(jnp.bfloat16),
    )


def hann(length, first, number):
    index = (first + jnp.arange(number, dtype=jnp.int32)).astype(jnp.float32)
    return 0.5 - 0.5 * jnp.cos(2.0 * math.pi / length * index)


def local(tiles, pairs, counts):
    row_count = lax.axis_size("rows")
    row_index = lax.axis_index("rows")
    tile_rows = tiles.shape[1]
    width = tiles.shape[2]
    height = tile_rows * row_count
    cos_h, sin_h = dft_tables(height)
    cos_w, sin_w = dft_tables(width)
    window = (
        hann(height, row_index * tile_rows, tile_rows)[:, None] * hann(width, 0, width)[None, :]
    )
    shaded = (tiles * window[None]).astype(jnp.bfloat16)
    y_real = jnp.einsum("grn,nv->grv", shaded, cos_w, preferred_element_type=jnp.float32).astype(
        jnp.bfloat16
    )
    y_imag = (-jnp.einsum("grn,nv->grv", shaded, sin_w, preferred_element_type=jnp.float32)).astype(
        jnp.bfloat16
    )
    stacked = jnp.stack([y_real, y_imag], axis=1)
    columns = lax.all_to_all(stacked, "rows", split_axis=3, concat_axis=2, tiled=True)
    f_real = jnp.einsum(
        "ur,grv->guv", cos_h, columns[:, 0], preferred_element_type=jnp.float32
    ) + jnp.einsum("ur,grv->guv", sin_h, columns[:, 1], preferred_element_type=jnp.float32)
    f_imag = jnp.einsum(
        "ur,grv->guv", cos_h, columns[:, 1], preferred_element_type=jnp.float32
    ) - jnp.einsum("ur,grv->guv", sin_h, columns[:, 0], preferred_element_type=jnp.float32)
    spectra = jnp.stack([f_real, f_imag], axis=1).astype(jnp.bfloat16)
    half_turn = lax.axis_size("blk") // 2
    partner = passed_along(spectra, "blk", half_turn)
    combined = jnp.concatenate([spectra, partner], axis=0)
    first = pairs[0, :, 0]
    second = pairs[0, :, 1]
    left = jnp.take(spectra, first, axis=0).astype(jnp.float32)
    right = jnp.take(combined, second, axis=0).astype(jnp.float32)
    cross_real = left[:, 0] * right[:, 0] + left[:, 1] * right[:, 1]
    cross_imag = left[:, 1] * right[:, 0] - left[:, 0] * right[:, 1]
    factor = 1.0 / (jnp.sqrt(cross_real * cross_real + cross_imag * cross_imag) + FLOOR)
    q_real = (cross_real * factor).astype(jnp.bfloat16)
    q_imag = (cross_imag * factor).astype(jnp.bfloat16)
    z_real = jnp.einsum(
        "ru,puv->prv", cos_h, q_real, preferred_element_type=jnp.float32
    ) - jnp.einsum("ru,puv->prv", sin_h, q_imag, preferred_element_type=jnp.float32)
    z_imag = jnp.einsum(
        "ru,puv->prv", sin_h, q_real, preferred_element_type=jnp.float32
    ) + jnp.einsum("ru,puv->prv", cos_h, q_imag, preferred_element_type=jnp.float32)
    half_done = jnp.stack([z_real, z_imag], axis=1).astype(jnp.bfloat16)
    banded = lax.all_to_all(half_done, "rows", split_axis=2, concat_axis=3, tiled=True)
    surface = jnp.einsum(
        "prv,vn->prn", banded[:, 0], cos_w, preferred_element_type=jnp.float32
    ) - jnp.einsum("prv,vn->prn", banded[:, 1], sin_w, preferred_element_type=jnp.float32)
    slot_index = jnp.arange(pairs.shape[1], dtype=jnp.int32)
    live = (slot_index < counts[0]).astype(jnp.float32)
    return surface * live[:, None, None]


def solution(mesh):
    return jax.shard_map(
        local,
        mesh=mesh,
        in_specs=(
            P(("parts", "blk"), "rows", None),
            P(("parts", "blk"), None, None),
            P(("parts", "blk")),
        ),
        out_specs=P(("parts", "blk"), "rows", None),
        check_vma=False,
    )
```

profile of v0, /device:TPU:1, one launch (start us, length us, event | category | flops | bytes accessed | tf_op | source)
XLA Modules:
  0.0 390.1 jit_solution(5445066731936324704)
XLA Ops:
  0.1 0.1 broadcast_multiply_fusion
  0.2 0.0 copy-start.5
  0.3 18.3 %fusion.55 = bf16[2,1,256,1024]{3,2,0,1:T(8,128)(2,1)S(1)} fusion(f32[2,256,1024]{2,1,0:T(8,128)} %param.3, f32[256,1024]{1,0:T(8,128)S(1)} %broadcast_multiply_fusion), kind=kOutput, calls=%fused_computation.58 | convolution fusion | flops 1092091904 | bytes 4194304 | tf_op jit(solution)/shard_map/grn,nv->grv/dot_general | solution.py:45
  18.6 0.0 copy-done.5
  18.6 17.0 %fusion.58 = bf16[2,1,256,1024]{3,2,0,1:T(8,128)(2,1)S(1)} fusion(f32[2,256,1024]{2,1,0:T(8,128)S(1)} %copy-done.5, f32[256,1024]{1,0:T(8,128)S(1)} %broadcast_multiply_fusion), kind=kOutput, calls=%fused_computation.59 | convolution fusion | flops 1092616192 | bytes 4194304 | tf_op jit(solution)/shard_map/grn,nv->grv/dot_general | solution.py:48
  35.6 0.2 pad_maximum_fusion.1
  35.8 4.0 %copy.20 = bf16[2,2,256,1024]{2,0,1,3:T(2,128)(2,1)} copy(bf16[2,2,256,1024]{3,2,0,1:T(8,128)(2,1)S(1)} %pad_maximum_fusion.1) | data formatting | bytes 4194304 | tf_op jit(solution)/shard_map/stack | solution.py:51
  39.8 28.9 %all_to_all.36 = bf16[2,2,256,1024]{2,0,1,3:T(2,128)(2,1)S(1)} all-to-all(bf16[2,2,256,1024]{2,0,1,3:T(2,128)(2,1)} %copy.20), channel_id=1, replica_groups=mesh['parts'=2,'blk'=4,'rows'=4] {'rows'}, dimensions={3} | all-to-all | bytes 4194304 | tf_op jit(solution)/shard_map/all_to_all | solution.py:52
  68.8 1.6 copy.35
  70.4 2.9 all_to_all.29
  73.2 0.0 copy-start.3
  73.2 18.0 %fusion.24 = f32[2,256,1024]{2,1,0:T(8,128)S(1)} fusion(bf16[2,2,1024,256]{2,3,0,1:T(8,128)(2,1)} %all_to_all.29), kind=kOutput, calls=%fused_computation.48 | convolution fusion | flops 1090519040 | bytes 3145728 | tf_op jit(solution)/shard_map/ur,grv->guv/dot_general | solution.py:55
  91.3 0.0 copy-done.3
  91.3 16.9 %fusion.22 = f32[2,256,1024]{2,1,0:T(8,128)S(1)} fusion(bf16[2,2,1024,256]{2,3,0,1:T(8,128)(2,1)S(1)} %copy-done.3), kind=kOutput, calls=%fused_computation.47 | convolution fusion | flops 1090519040 | bytes 3145728 | tf_op jit(solution)/shard_map/ur,grv->guv/dot_general | solution.py:58
  108.2 16.8 %fusion.61 = bf16[2,1,1024,256]{2,3,0,1:T(8,128)(2,1)S(1)} fusion(f32[2,256,1024]{2,1,0:T(8,128)S(1)} %fusion.24, bf16[2,2,1024,256]{2,3,0,1:T(8,128)(2,1)S(1)} %copy-done.3), kind=kOutput, calls=%fused_computation.60 | convolution fusion | flops 1091567616 | bytes 4194304 | tf_op jit(solution)/shard_map/ur,grv->guv/dot_general | solution.py:53
  124.9 16.8 %fusion.64 = bf16[2,1,1024,256]{2,3,0,1:T(8,128)(2,1)S(1)} fusion(f32[2,256,1024]{2,1,0:T(8,128)S(1)} %fusion.22, bf16[2,2,1024,256]{2,3,0,1:T(8,128)(2,1)S(1)} %copy-done.3), kind=kOutput, calls=%fused_computation.61 | convolution fusion | flops 1091567616 | bytes 4194304 | tf_op jit(solution)/shard_map/ur,grv->guv/dot_general | solution.py:56
  141.8 0.0 copy-start.1
  141.8 0.0 copy-start.4
  141.8 1.6 pad_maximum_fusion.2
  143.4 3.1 collective-permute-start
  146.6 0.0 copy-done.4
  146.6 0.2 slice_reduce_fusion.1
  146.8 0.0 copy-done.1
  146.8 2.9 copy.22
  149.7 2.0 gather_fusion
  151.7 3.0 copy.23
  154.7 0.0 copy-start.2
  154.7 2.3 select_convert_fusion.1
  157.0 79.8 %collective-permute-done = bf16[2,2,1024,256]{2,3,0,1:T(8,128)(2,1)} collective-permute-done((bf16[2,2,1024,256]{2,3,0,1:T(8,128)(2,1)}, bf16[2,2,1024,256]{2,3,0,1:T(8,128)(2,1)}, u32[]{:S(2)}, u32[]{:S(2)}) %collective-permute-start) | collective-permute-done | bytes 2097184 | tf_op jit(solution)/shard_map/ppermute | solution.py:14
  236.8 0.0 copy-done.2
  236.8 3.8 pad_maximum_fusion
  240.7 2.9 gather_fusion.1
  243.5 0.3 select_convert_fusion
  243.9 1.8 copy-done
  245.7 1.6 fusion.12
  247.3 16.8 %fusion.20 = f32[2,256,1024]{2,1,0:T(8,128)S(1)} fusion(bf16[2,1024,256]{1,2,0:T(8,128)(2,1)S(1)} %get-tuple-element.7), kind=kOutput, calls=%fused_computation.46 | convolution fusion | flops 1090519040 | bytes 3145728 | tf_op jit(solution)/shard_map/ru,puv->prv/dot_general | solution.py:74
  264.1 0.9 fusion.14
  265.1 16.8 %fusion.18 = f32[2,256,1024]{2,1,0:T(8,128)S(1)} fusion(bf16[2,1024,256]{1,2,0:T(8,128)(2,1)S(1)} %fusion.14), kind=kOutput, calls=%fused_computation.45 | convolution fusion | flops 1090519040 | bytes 3145728 | tf_op jit(solution)/shard_map/ru,puv->prv/dot_general | solution.py:75
  281.9 16.7 %fusion.67 = bf16[2,1,1024,256]{2,3,0,1:T(8,128)(2,1)S(1)} fusion(f32[2,256,1024]{2,1,0:T(8,128)S(1)} %fusion.20, bf16[2,1024,256]{1,2,0:T(8,128)(2,1)S(1)} %fusion.14), kind=kOutput, calls=%fused_computation.62 | convolution fusion | flops 1091567616 | bytes 4194304 | tf_op jit(solution)/shard_map/ru,puv->prv/dot_general | solution.py:72
  298.6 16.5 %fusion.70 = bf16[2,1,1024,256]{2,3,0,1:T(8,128)(2,1)S(1)} fusion(f32[2,256,1024]{2,1,0:T(8,128)S(1)} %fusion.18, bf16[2,1024,256]{1,2,0:T(8,128)(2,1)S(1)} %get-tuple-element.7), kind=kOutput, calls=%fused_computation.63 | convolution fusion | flops 1091567616 | bytes 4194304 | tf_op jit(solution)/shard_map/ru,puv->prv/dot_general | solution.py:77
  315.1 0.2 pad_maximum_fusion.3
  315.3 4.0 %copy.29 = bf16[2,2,1024,256]{3,0,1,2:T(2,128)(2,1)} copy(bf16[2,2,1024,256]{2,3,0,1:T(8,128)(2,1)S(1)} %pad_maximum_fusion.3) | data formatting | bytes 4194304 | tf_op jit(solution)/shard_map/stack | solution.py:78
  319.4 5.2 %all-to-all-start.1 = ((bf16[2,2,1024,256]{3,0,1,2:T(2,128)(2,1)}), bf16[2,2,1024,256]{3,0,1,2:T(2,128)(2,1)S(1)}, u32[]{:S(2)}, u32[]{:S(2)}) async-start(bf16[2,2,1024,256]{3,0,1,2:T(2,128)(2,1)} %copy.29), calls=%async_computation.1 | async-start | bytes 4194304 | tf_op jit(solution)/shard_map/all_to_all | solution.py:79
  325.2 24.2 %all-to-all-done.1 = bf16[2,2,1024,256]{3,0,1,2:T(2,128)(2,1)S(1)} async-done(((bf16[2,2,1024,256]{3,0,1,2:T(2,128)(2,1)}), bf16[2,2,1024,256]{3,0,1,2:T(2,128)(2,1)S(1)}, u32[]{:S(2)}, u32[]{:S(2)}) %all-to-all-start.1) | async-done | bytes 2097184 | tf_op jit(solution)/shard_map/all_to_all | solution.py:79
  349.4 2.9 copy.34
  352.3 3.6 all_to_all.33
  355.9 16.5 %fusion.16 = f32[2,256,1024]{2,1,0:T(8,128)S(1)} fusion(bf16[2,2,256,1024]{3,2,0,1:T(8,128)(2,1)S(1)} %all_to_all.33), kind=kOutput, calls=%fused_computation.44 | convolution fusion | flops 1090519040 | bytes 3145728 | tf_op jit(solution)/shard_map/prv,vn->prn/dot_general | solution.py:82
  372.4 17.5 %subtract_multiply_fusion = f32[2,256,1024]{2,1,0:T(8,128)} fusion(f32[2,256,1024]{2,1,0:T(8,128)S(1)} %fusion.16, bf16[2,2,256,1024]{3,2,0,1:T(8,128)(2,1)S(1)} %all_to_all.33, f32[2]{0:T(128)S(1)} %compare_convert_fusion), kind=kOutput, calls=%fused_computation.36 | convolution fusion | flops 1091567616 | bytes 5243392 | tf_op jit(solution)/shard_map/prv,vn->prn/dot_general | solution.py:80
  (9 shorter events, 0.1 us)
Async XLA Ops:
  0.2 18.3 %copy-start.5 = (f32[2,256,1024]{2,1,0:T(8,128)S(1)}, f32[2,256,1024]{2,1,0:T(8,128)}, u32[]{:S(2)}) copy-start(f32[2,256,1024]{2,1,0:T(8,128)} %param.3) | copy-start | bytes 6291460
  73.2 18.1 %copy-start.3 = (bf16[2,2,1024,256]{2,3,0,1:T(8,128)(2,1)S(1)}, bf16[2,2,1024,256]{2,3,0,1:T(8,128)(2,1)}, u32[]{:S(2)}) copy-start(bf16[2,2,1024,256]{2,3,0,1:T(8,128)(2,1)} %all_to_all.29) | copy-start | bytes 6291460
  141.8 5.0 %copy-start.1 = (bf16[2,1,1024,256]{2,3,0,1:T(8,128)(2,1)}, bf16[2,1,1024,256]{2,3,0,1:T(8,128)(2,1)S(1)}, u32[]{:S(2)}) copy-start(bf16[2,1,1024,256]{2,3,0,1:T(8,128)(2,1)S(1)} %fusion.64) | copy-start | bytes 3145732
  141.8 4.8 %copy-start.4 = (s32[1,2,2]{2,1,0:T(2,128)S(1)}, s32[1,2,2]{2,1,0:T(2,128)}, u32[]{:S(2)}) copy-start(s32[1,2,2]{2,1,0:T(2,128)} %param.4) | copy-start | bytes 52
  143.4 93.4 %collective-permute-start = (bf16[2,2,1024,256]{2,3,0,1:T(8,128)(2,1)}, bf16[2,2,1024,256]{2,3,0,1:T(8,128)(2,1)}, u32[]{:S(2)}, u32[]{:S(2)}) collective-permute-start(bf16[2,2,1024,256]{2,3,0,1:T(8,128)(2,1)} %pad_maximum_fusion.2), channel_id=1, source_target_pairs={{0,8},{4,12},{8,0},{12,4},{1,9},{5,13},{9,1},{13,5},{2,10},{6,14},... | collective-permute-start | bytes 6291464 | tf_op jit(solution)/shard_map/ppermute | solution.py:14
  154.7 82.1 %copy-start.2 = (bf16[2,1,1024,256]{2,3,0,1:T(8,128)(2,1)S(1)}, bf16[2,1,1024,256]{2,3,0,1:T(8,128)(2,1)}, u32[]{:S(2)}) copy-start(bf16[2,1,1024,256]{2,3,0,1:T(8,128)(2,1)} %copy-done.1) | copy-start | bytes 3145732
  243.5 2.2 copy-start
  319.4 30.0 %all-to-all-start.1 = ((bf16[2,2,1024,256]{3,0,1,2:T(2,128)(2,1)}), bf16[2,2,1024,256]{3,0,1,2:T(2,128)(2,1)S(1)}, u32[]{:S(2)}, u32[]{:S(2)}) async-start(bf16[2,2,1024,256]{3,0,1,2:T(2,128)(2,1)} %copy.29), calls=%async_computation.1 | async-start | bytes 4194304 | tf_op jit(solution)/shard_map/all_to_all | solution.py:79
where the time goes:
time: 398 us; the launch traced here: 390 us
  matrix products  205 us (52%)
  waiting for transfers between devices  104 us (26%)
  local copies, waits for them, and re-layouts  31.9 us (8%)
  blocking collectives  28.9 us (7%)
  other arithmetic  11.3 us (3%)
  starting transfers between devices  8.3 us (2%)
    ppermute x1, waiting for transfers between devices, passed_along(): return lax.ppermute(value, axis, pairs)  79.8 us
    all_to_all x1, blocking collectives, local(): lax.all_to_all(stacked, 'rows', split_axis=3, concat_axis=2, tiled=True)  28.9 us
    all_to_all x1, waiting for transfers between devices, local(): lax.all_to_all(half_done, 'rows', split_axis=2, concat_axis=3, tiled=True)  24.2 us
    dot_general x1, matrix products, local(): jnp.einsum('grn,nv->grv', shaded, cos_w, preferred_element_type=jnp.float32)  18.3 us
    dot_general x1, matrix products, local(): jnp.einsum('ur,grv->guv', sin_h, columns[:, 1], preferred_element_type=jn...  18 us
    dot_general x1, matrix products, local(): jnp.einsum('prv,vn->prn', banded[:, 0], cos_w, preferred_element_type=jnp...  17.5 us
    dot_general x1, matrix products, local(): jnp.einsum('grn,nv->grv', shaded, sin_w, preferred_element_type=jnp.float32)  17 us
    dot_general x1, matrix products, local(): jnp.einsum('ur,grv->guv', sin_h, columns[:, 0], preferred_element_type=jn...  16.9 us
  transfers between devices with their start and end apart: 2, of which 2 were waited for; matrix products, arithmetic and copies ran while one was open for 3% of the time, Pallas kernels for 0%

commit v1 on v0

v1 whole, which is shorter than its diff:
```python
import functools
import math

import jax
import jax.numpy as jnp
import ml_dtypes
import numpy as np
from jax import lax
from jax.experimental import pallas as pl
from jax.experimental.pallas import tpu as pltpu
from jax.sharding import PartitionSpec as P

FLOOR = 0.05
LANES = 128
MESH = pl.DeviceIdType.MESH
BF16 = jnp.bfloat16
F32 = jnp.float32


def dft_tables(length):
    index = np.arange(length)
    angle = 2.0 * math.pi / length * (index[:, None] * index[None, :] % length)
    factor = 1.0 / math.sqrt(length)
    return (
        (np.cos(angle) * factor).astype(ml_dtypes.bfloat16).astype(np.float32),
        (np.sin(angle) * factor).astype(ml_dtypes.bfloat16).astype(np.float32),
    )


def hann(length):
    return (0.5 - 0.5 * np.cos(2.0 * math.pi / length * np.arange(length))).astype(np.float32)


def row_tables(width, n, width_chunk):
    cos_w, sin_w = dft_tables(width)
    half = width // 2
    real, imag = cos_w[:, :half].copy(), -sin_w[:, :half]
    imag[:, 0] = cos_w[:, half]
    forward = np.stack([real, imag], 1).reshape(width, 2, n, -1, width_chunk).transpose(3, 0, 2, 1, 4)
    inverse_real, inverse_imag = 2.0 * real, 2.0 * imag
    inverse_real[:, 0], inverse_imag[:, 0] = real[:, 0], imag[:, 0]
    inverse = np.stack([inverse_real, inverse_imag], 1).reshape(width, 2, n, -1, width_chunk).transpose(3, 2, 1, 4, 0)
    chunks = half // n // width_chunk
    return (
        forward.reshape(chunks, width, n * 2 * width_chunk).astype(ml_dtypes.bfloat16),
        inverse.reshape(chunks, n * 2 * width_chunk, width).astype(ml_dtypes.bfloat16),
    )


def mm(a, b):
    return jnp.dot(a, b, preferred_element_type=F32)


def kernel(
    n, nb, cw,
    pairs, counts, tiles_hbm, hann_h, hann_w, fwd_hbm, cos_hbm, sin_hbm, inv_hbm,
    out,
    tiles, fwd, cos, sin, inv, shaded, fsend, frecv, ops, spec, pspec, qfix, zsend, zrecv,
    load_sem, fs, fr, zs, zr, bs, br,
):
    me = lax.axis_index("rows")
    blk = lax.axis_index("blk")
    partner = lax.rem(blk + nb // 2, nb)
    groups, band, width = tiles.shape
    height = cos.shape[0]
    chunks = spec.shape[0]
    step = min(256, height // 2)
    steps = height // step
    block = LANES // 2

    loads = [
        pltpu.make_async_copy(src, dst, load_sem.at[i])
        for i, (src, dst) in enumerate(
            [(tiles_hbm, tiles), (fwd_hbm, fwd), (cos_hbm, cos), (sin_hbm, sin), (inv_hbm, inv)]
        )
    ]
    for load in loads:
        load.start()

    barrier = pltpu.get_barrier_semaphore()
    for k in range(1, n):
        pl.semaphore_signal(barrier, inc=1, device_id={"rows": lax.rem(me + k, n)}, device_id_type=MESH)
    pl.semaphore_signal(barrier, inc=1, device_id={"blk": partner}, device_id_type=MESH)

    def lanes_of(rows):
        return lax.broadcasted_iota(jnp.int32, (rows, LANES), 1)

    def is_re_of(rows):
        return lax.rem(lanes_of(rows), 2 * cw) < cw

    def shared_of(rows):
        return lax.rem(lanes_of(rows), cw) == jnp.where(me == 0, 0, -1)

    def swap(x):
        return jnp.where(is_re_of(x.shape[0]), pltpu.roll(x, LANES - cw, 1), pltpu.roll(x, cw, 1))

    def forward_copy(j, k):
        return pltpu.make_async_remote_copy(
            src_ref=fsend.at[j, lax.rem(me + k, n)],
            dst_ref=frecv.at[j, pl.ds(pl.multiple_of(me * band, band), band)],
            send_sem=fs.at[j, k - 1],
            recv_sem=fr.at[j, k - 1],
            device_id={"rows": lax.rem(me + k, n)},
            device_id_type=MESH,
        )

    def partner_copy(j):
        return pltpu.make_async_remote_copy(
            src_ref=spec.at[j],
            dst_ref=pspec.at[j],
            send_sem=zs.at[j],
            recv_sem=zr.at[j],
            device_id={"blk": partner},
            device_id_type=MESH,
        )

    def back_copy(j, k):
        return pltpu.make_async_remote_copy(
            src_ref=zsend.at[j, pl.ds(pl.multiple_of(lax.rem(me + k, n) * band, band), band)],
            dst_ref=zrecv.at[j, me],
            send_sem=bs.at[j, k - 1],
            recv_sem=br.at[j, k - 1],
            device_id={"rows": lax.rem(me + k, n)},
            device_id_type=MESH,
        )

    loads[0].wait()
    for g in range(groups):
        shaded[g] = (tiles[g] * (hann_h[...] * hann_w[...])).astype(BF16)
    loads[1].wait()
    low = lanes_of(band) < block
    for j in range(chunks):
        first = mm(shaded[0], fwd[j])
        second = mm(shaded[1], fwd[j])
        for m in range(n // 2):
            a = first[:, m * LANES : (m + 1) * LANES]
            b = second[:, m * LANES : (m + 1) * LANES]
            fsend[j, 2 * m] = jnp.where(low, a, pltpu.roll(b, block, 1)).astype(BF16)
            fsend[j, 2 * m + 1] = jnp.where(low, pltpu.roll(a, block, 1), b).astype(BF16)
        if j == 0:
            pl.semaphore_wait(barrier, n)
        for k in range(1, n):
            forward_copy(j, k).start()
        frecv[j, pl.ds(pl.multiple_of(me * band, band), band)] = fsend[j, me]

    loads[2].wait()
    loads[3].wait()
    for j in range(chunks):
        for k in range(1, n):
            forward_copy(j, k).wait_recv()
        for half in range(2 if j == 0 else 1):

            def operands(i, _, half=half, j=j):
                at = pl.ds(pl.multiple_of(i * step, step), step)
                y = frecv[j, at].astype(F32)
                is_re, shared = is_re_of(step), shared_of(step)
                if j == 0:
                    y = jnp.where(shared, jnp.where(is_re, swap(y) if half else y, 0.0), y)
                other = swap(y)
                ops[half, 0, at] = y.astype(BF16)
                ops[half, 1, at] = jnp.where(is_re, other, -other).astype(BF16)
                return 0

            lax.fori_loop(0, steps, operands, 0)
        for half in range(2):
            use = half if j == 0 else 0

            def columns(i, _, use=use, j=j):
                at = pl.ds(pl.multiple_of(i * step, step), step)
                spec[j, at] = (mm(cos[at], ops[use, 0]) + mm(sin[at], ops[use, 1])).astype(BF16)
                return 0

            lax.fori_loop(half * steps // 2, (half + 1) * steps // 2, columns, 0)
        if j == 0:
            middle = height // 2
            rows = lax.broadcasted_iota(jnp.int32, (16, LANES), 0)
            mark = (rows == 0) & shared_of(16) & ~is_re_of(16)
            top = swap(mm(cos[middle : middle + 16], ops[0, 0]))
            bottom = swap(mm(cos[0:16], ops[1, 0]))
            spec[0, 0:16] = jnp.where(mark, top, spec[0, 0:16].astype(F32)).astype(BF16)
            spec[0, middle : middle + 16] = jnp.where(
                mark, bottom, spec[0, middle : middle + 16].astype(F32)
            ).astype(BF16)
        partner_copy(j).start()

    def gather(j):
        for k in range(1, n):
            back_copy(j, k).wait_recv()
        parts = [[], []]
        for m in range(n // 2):
            a = zrecv[j, 2 * m].astype(F32)
            b = zrecv[j, 2 * m + 1].astype(F32)
            parts[0].append(jnp.where(low, a, pltpu.roll(b, block, 1)).astype(BF16))
            parts[1].append(jnp.where(low, pltpu.roll(a, block, 1), b).astype(BF16))
        for p in range(2):
            z = jnp.concatenate(parts[p], axis=1)
            scale = jnp.where(p < counts[0], 1.0, 0.0).astype(F32)
            for c in range(0, width, 256):
                value = mm(z, inv[j, :, c : c + 256])
                if j > 0:
                    value = out[p, :, c : c + 256] + value
                if j == chunks - 1:
                    value = value * scale
                out[p, :, c : c + 256] = value

    for j in range(chunks):
        partner_copy(j).wait_recv()

        def cross(i, _, j=j, bottom=False):
            at = pl.ds(pl.multiple_of(i * step, step), step)
            is_re = is_re_of(step)
            slot_low = lanes_of(step) < block
            own = spec[j, at].astype(F32)
            far = pspec[j, at].astype(F32)
            own_turned = pltpu.roll(own, block, 1)
            far_turned = pltpu.roll(far, block, 1)
            want_left = jnp.where(slot_low, pairs[0], 1 - pairs[2])
            want_right = jnp.where(slot_low, lax.rem(pairs[1], 2), 1 - lax.rem(pairs[3], 2))
            want_far = jnp.where(slot_low, pairs[1], pairs[3]) >= 2
            left = jnp.where(want_left == 0, own, own_turned)
            right = jnp.where(
                want_right == 0, jnp.where(want_far, far, own), jnp.where(want_far, far_turned, own_turned)
            )
            left_other, right_other = swap(left), swap(right)
            crossed = jnp.where(
                is_re, left * right + left_other * right_other, left * right_other - left_other * right
            )
            crossed_other = swap(crossed)
            power = crossed * crossed + crossed_other * crossed_other
            if j == 0:
                shared = shared_of(step)
                rows = lax.broadcasted_iota(jnp.int32, (step, LANES), 0) + i * step
                single = shared & (lax.rem(rows, height // 2) == 0)
                crossed = jnp.where(single, left * right, crossed)
                power = jnp.where(single, crossed * crossed, power)
            q = (crossed / (jnp.sqrt(power) + FLOOR)).astype(BF16).astype(F32)
            other = swap(q)
            for_cos, for_sin = q, jnp.where(is_re, -other, other)
            if j == 0:
                weight = jnp.where(single, 1.0, 2.0)
                if bottom:
                    for_cos = jnp.where(shared, jnp.where(is_re, 0.0, weight * other), for_cos)
                    for_sin = jnp.where(shared, jnp.where(is_re, 0.0, -2.0 * q), for_sin)
                else:
                    for_cos = jnp.where(shared, jnp.where(is_re, weight * q, 0.0), for_cos)
                    for_sin = jnp.where(shared, jnp.where(is_re, -2.0 * other, 0.0), for_sin)

                @pl.when(lax.rem(i, steps // 2) == 0)
                def _():
                    qfix[1 if bottom else 0] = q[0:16]

            ops[0, 0, at] = for_cos.astype(BF16)
            ops[0, 1, at] = for_sin.astype(BF16)
            return 0

        lax.fori_loop(0, steps // 2, functools.partial(cross, bottom=False), 0)
        lax.fori_loop(steps // 2, steps, functools.partial(cross, bottom=True), 0)
        if j == 0:
            middle = height // 2
            rows = lax.broadcasted_iota(jnp.int32, (16, LANES), 0)
            mark = (rows == 0) & shared_of(16)
            is_re = is_re_of(16)
            ops[0, 0, 0:16] = jnp.where(mark & ~is_re, qfix[1], ops[0, 0, 0:16].astype(F32)).astype(BF16)
            ops[0, 0, middle : middle + 16] = jnp.where(
                mark & is_re, swap(qfix[0]), ops[0, 0, middle : middle + 16].astype(F32)
            ).astype(BF16)

        def inverse(i, _, j=j):
            at = pl.ds(pl.multiple_of(i * step, step), step)
            zsend[j, at] = (mm(cos[at], ops[0, 0]) + mm(sin[at], ops[0, 1])).astype(BF16)
            return 0

        lax.fori_loop(0, steps, inverse, 0)
        for k in range(1, n):
            back_copy(j, k).start()
        zrecv[j, me] = zsend[j, pl.ds(pl.multiple_of(me * band, band), band)]
        if j == 0:
            loads[4].wait()
        else:
            gather(j - 1)
    gather(chunks - 1)

    for j in range(chunks):
        for k in range(1, n):
            forward_copy(j, k).wait_send()
            back_copy(j, k).wait_send()
        partner_copy(j).wait_send()


def local(tiles, pairs, counts):
    n = lax.axis_size("rows")
    nb = lax.axis_size("blk")
    groups, band, width = tiles.shape
    slots = pairs.shape[1]
    height = band * n
    cw = LANES // (2 * groups)
    chunks = width // 2 // n // cw
    cos_h, sin_h = dft_tables(height)
    forward, inverse = row_tables(width, n, cw)
    rows = lax.dynamic_slice(jnp.asarray(hann(height)), (lax.axis_index("rows") * band,), (band,))
    vmem = pl.BlockSpec(memory_space=pltpu.VMEM)
    smem = pl.BlockSpec(memory_space=pltpu.SMEM)
    hbm = pl.BlockSpec(memory_space=pl.ANY)
    dma = pltpu.SemaphoreType.DMA
    return pl.pallas_call(
        functools.partial(kernel, n, nb, cw),
        out_shape=jax.ShapeDtypeStruct((slots, band, width), F32),
        in_specs=[smem, smem, hbm, vmem, vmem, hbm, hbm, hbm, hbm],
        out_specs=vmem,
        scratch_shapes=[
            pltpu.VMEM(tiles.shape, F32),
            pltpu.VMEM(forward.shape, BF16),
            pltpu.VMEM((height, height), BF16),
            pltpu.VMEM((height, height), BF16),
            pltpu.VMEM(inverse.shape, BF16),
            pltpu.VMEM(tiles.shape, BF16),
            pltpu.VMEM((chunks, n, band, LANES), BF16),
            pltpu.VMEM((chunks, height, LANES), BF16),
            pltpu.VMEM((2, 2, height, LANES), BF16),
            pltpu.VMEM((chunks, height, LANES), BF16),
            pltpu.VMEM((chunks, height, LANES), BF16),
            pltpu.VMEM((2, 16, LANES), F32),
            pltpu.VMEM((chunks, height, LANES), BF16),
            pltpu.VMEM((chunks, n, band, LANES), BF16),
            dma((5,)),
            dma((chunks, n - 1)),
            dma((chunks, n - 1)),
            dma((chunks,)),
            dma((chunks,)),
            dma((chunks, n - 1)),
            dma((chunks, n - 1)),
        ],
        compiler_params=pltpu.CompilerParams(
            collective_id=0, has_side_effects=True, vmem_limit_bytes=48 * 1024 * 1024
        ),
    )(
        pairs.reshape(-1),
        counts,
        tiles,
        rows[:, None],
        jnp.asarray(hann(width))[None, :],
        jnp.asarray(forward),
        jnp.asarray(cos_h.astype(ml_dtypes.bfloat16)),
        jnp.asarray(sin_h.astype(ml_dtypes.bfloat16)),
        jnp.asarray(inverse),
    )


def solution(mesh):
    return jax.shard_map(
        local,
        mesh=mesh,
        in_specs=(
            P(("parts", "blk"), "rows", None),
            P(("parts", "blk"), None, None),
            P(("parts", "blk")),
        ),
        out_specs=P(("parts", "blk"), "rows", None),
        check_vma=False,
    )
```

time: 398 us -> 75.1 us (0.19); the launches traced: 390 us -> 74.8 us
  matrix products: 205 us -> 0 us
  waiting for transfers between devices: 104 us -> 0 us
  Pallas kernels: 0 us -> 68.9 us
  blocking collectives: 28.9 us -> 0 us
  local copies, waits for them, and re-layouts: 31.9 us -> 5.25 us
  other arithmetic: 11.3 us -> 0 us
  starting transfers between devices: 8.3 us -> 0 us
    dot_general x12 -> x0, matrix products: 205 us -> none  [the longest x1 18.3 us: local(): jnp.einsum('grn,nv->grv', shaded, cos_w, preferred_element_type=jnp.float32)]
    ppermute x1 -> x0, waiting for transfers between devices: 79.8 us -> none  [passed_along(): return lax.ppermute(value, axis, pairs)]
    pallas_call x0 -> x1, Pallas kernels: none -> 68.9 us  [local(): pl.pallas_call(functools.partial(kernel, n, nb, cw), out_shape=jax.ShapeD...]
    all_to_all x1 -> x0, blocking collectives: 28.9 us -> none  [local(): lax.all_to_all(stacked, 'rows', split_axis=3, concat_axis=2, tiled=True)]
    all_to_all x1 -> x0, waiting for transfers between devices: 24.2 us -> none  [local(): lax.all_to_all(half_done, 'rows', split_axis=2, concat_axis=3, tiled=True)]
    all_to_all x4 -> x0, local copies, waits for them, and re-layouts: 11 us -> none  [the longest x2 6.57 us: local(): lax.all_to_all(half_done, 'rows', split_axis=2, concat_axis=3, tiled=True)]
    another operation x3 -> x0, local copies, waits for them, and re-layouts: 11 us -> none  [the longest x1 4.05 us: local(): stacked = jnp.stack([y_real, y_imag], axis=1)]
    gather x3 -> x0, local copies, waits for them, and re-layouts: 7.89 us -> none  [the longest x2 5.02 us: local(): left = jnp.take(spectra, first, axis=0).astype(jnp.float32)]
  transfers between devices with their start and end apart: 2 -> 0, of which waited for: 2 -> 0; matrix products, arithmetic and copies ran while one was open for 3% -> 0% of each run, Pallas kernels for 0% -> 0%
where the time goes in v1:
time: 75.1 us; the launch traced here: 74.8 us
  Pallas kernels  68.9 us (92%)
  local copies, waits for them, and re-layouts  5.25 us (7%)
    pallas_call x1, Pallas kernels, local(): pl.pallas_call(functools.partial(kernel, n, nb, cw), out_shape=jax.ShapeD...  68.9 us
    unnamed x5, local copies, waits for them, and re-layouts  3.6 us

profile of v1, /device:TPU:1, one launch (start us, length us, event | category | flops | bytes accessed | tf_op | source)
XLA Modules:
  0.0 74.8 jit_solution(8792885805716344749)
XLA Ops:
  0.7 0.8 %dynamic_slice.3 = f32[256]{0:T(256)S(1)} dynamic-slice(f32[1024]{0:T(1024)} %constant.20.clone, s32[]{:T(128)S(6)} %select_n.3), dynamic_slice_sizes={256} | dynamic-slice | bytes 2052 | tf_op jit(solution)/shard_map/dynamic_slice | solution.py:300
  1.4 0.8 %reshape.3.pairs = s32[4]{0:T(128)S(1)} reshape(s32[1,2,2]{2,1,0:T(2,128)} %param.10) | data formatting | bytes 32 | tf_op jit(solution)/shard_map/reshape | solution.py:337
  2.2 0.1 copy.10.hann_h
  2.3 0.0 copy-start
  2.3 1.6 %copy-done = f32[2,256,1024]{2,1,0:T(8,128)S(1)} copy-done((f32[2,256,1024]{2,1,0:T(8,128)S(1)}, f32[2,256,1024]{2,1,0:T(8,128)}, u32[]{:S(2)}) %copy-start) | copy-done | bytes 2097176
  3.9 0.0 copy-start.1
  3.9 0.7 copy-done.1
  4.6 68.9 %shard_map.91 = f32[2,256,1024]{2,1,0:T(8,128)S(1)} custom-call(s32[4]{0:T(128)S(1)} %reshape.3.pairs, s32[1]{0:T(128)S(6)} %copy.12.counts, f32[2,256,1024]{2,1,0:T(8,128)S(1)} %copy-done, f32[256,1]{1,0:T(8,128)S(1)} %copy.10.hann_h, f32[1,1024]{1,0:T(1,128)S(1)} %copy-done.1, bf16[4,1024,256]{2,1,0:T(8,128)(2,1)} %constant.21.clone.fwd_hbm, ...), custom_call_target="tpu_custom_call" | custom-call | tf_op jit(solution)/shard_map/pallas_call | solution.py:305
  73.5 1.3 %copy.13 = f32[2,256,1024]{2,1,0:T(8,128)} copy(f32[2,256,1024]{2,1,0:T(8,128)S(1)} %shard_map.91) | data formatting | bytes 4194304
Async XLA Ops:
  2.3 1.6 %copy-start = (f32[2,256,1024]{2,1,0:T(8,128)S(1)}, f32[2,256,1024]{2,1,0:T(8,128)}, u32[]{:S(2)}) copy-start(f32[2,256,1024]{2,1,0:T(8,128)} %tiles_hbm.1) | copy-start | bytes 6291460
  3.9 0.7 copy-start.1

commit v2 on v1

--- a/solution.py
+++ b/solution.py
@@ -53,10 +53,10 @@
 
 def kernel(
     n, nb, cw,
-    pairs, counts, tiles_hbm, hann_h, hann_w, fwd_hbm, cos_hbm, sin_hbm, inv_hbm,
-    out,
-    tiles, fwd, cos, sin, inv, shaded, fsend, frecv, ops, spec, pspec, qfix, zsend, zrecv,
-    load_sem, fs, fr, zs, zr, bs, br,
+    pairs, counts, tiles_hbm, hann_hbm, hann_w, fwd_hbm, cos_hbm, sin_hbm, inv_hbm,
+    out_hbm,
+    out, tiles, hann_h, fwd, cos, sin, inv, shaded, fsend, frecv, far, ops, spec, pspec, qfix, zsum, zsend, zrecv,
+    load_sem, out_sem, fs, fr, gs, gr, zs, zr, bs, br,
 ):
     me = lax.axis_index("rows")
     blk = lax.axis_index("blk")
@@ -67,11 +67,13 @@
     step = min(256, height // 2)
     steps = height // step
     block = LANES // 2
+    middle = height // 2
+    order = [n // 2] + [k for k in range(1, n) if k != n // 2]
 
     loads = [
         pltpu.make_async_copy(src, dst, load_sem.at[i])
         for i, (src, dst) in enumerate(
-            [(tiles_hbm, tiles), (fwd_hbm, fwd), (cos_hbm, cos), (sin_hbm, sin), (inv_hbm, inv)]
+            [(tiles_hbm, tiles), (hann_hbm.at[me], hann_h), (fwd_hbm, fwd), (cos_hbm, cos), (sin_hbm, sin), (inv_hbm, inv)]
         )
     ]
     for load in loads:
@@ -80,7 +82,10 @@
     barrier = pltpu.get_barrier_semaphore()
     for k in range(1, n):
         pl.semaphore_signal(barrier, inc=1, device_id={"rows": lax.rem(me + k, n)}, device_id_type=MESH)
-    pl.semaphore_signal(barrier, inc=1, device_id={"blk": partner}, device_id_type=MESH)
+    for k in range(n):
+        pl.semaphore_signal(
+            barrier, inc=1, device_id={"blk": partner, "rows": lax.rem(me + k, n)}, device_id_type=MESH
+        )
 
     def lanes_of(rows):
         return lax.broadcasted_iota(jnp.int32, (rows, LANES), 1)
@@ -104,15 +109,29 @@
             device_id_type=MESH,
         )
 
-    def partner_copy(j):
+    def far_copy(k):
         return pltpu.make_async_remote_copy(
-            src_ref=spec.at[j],
-            dst_ref=pspec.at[j],
-            send_sem=zs.at[j],
-            recv_sem=zr.at[j],
+            src_ref=fsend.at[0, lax.rem(me + k, n)],
+            dst_ref=far.at[pl.ds(pl.multiple_of(me * band, band), band)],
+            send_sem=gs.at[k],
+            recv_sem=gr.at[k],
+            device_id={"blk": partner, "rows": lax.rem(me + k, n)},
+            device_id_type=MESH,
+        )
+
+    def partner_copy(j, half):
+        at = pl.ds(half * middle, middle)
+        return pltpu.make_async_remote_copy(
+            src_ref=spec.at[j, at],
+            dst_ref=pspec.at[j, at],
+            send_sem=zs.at[j, half],
+            recv_sem=zr.at[j, half],
             device_id={"blk": partner},
             device_id_type=MESH,
         )
+
+    def store(p):
+        return pltpu.make_async_copy(out.at[p], out_hbm.at[p], out_sem.at[p])
 
     def back_copy(j, k):
         return pltpu.make_async_remote_copy(
@@ -125,11 +144,13 @@
         )
 
     loads[0].wait()
+    loads[1].wait()
     for g in range(groups):
-        shaded[g] = (tiles[g] * (hann_h[...] * hann_w[...])).astype(BF16)
-    loads[1].wait()
+        shaded[g] = (tiles[g] * (hann_h[:, 0:1] * hann_w[...])).astype(BF16)
+    loads[2].wait()
     low = lanes_of(band) < block
-    for j in range(chunks):
+
+    def rows_to_columns(j):
         first = mm(shaded[0], fwd[j])
         second = mm(shaded[1], fwd[j])
         for m in range(n // 2):
@@ -137,25 +158,17 @@
             b = second[:, m * LANES : (m + 1) * LANES]
             fsend[j, 2 * m] = jnp.where(low, a, pltpu.roll(b, block, 1)).astype(BF16)
             fsend[j, 2 * m + 1] = jnp.where(low, pltpu.roll(a, block, 1), b).astype(BF16)
-        if j == 0:
-            pl.semaphore_wait(barrier, n)
-        for k in range(1, n):
-            forward_copy(j, k).start()
         frecv[j, pl.ds(pl.multiple_of(me * band, band), band)] = fsend[j, me]
 
-    loads[2].wait()
-    loads[3].wait()
-    for j in range(chunks):
-        for k in range(1, n):
-            forward_copy(j, k).wait_recv()
-        for half in range(2 if j == 0 else 1):
-
-            def operands(i, _, half=half, j=j):
+    def transform(source, target, shares):
+        for half in range(2 if shares else 1):
+
+            def operands(i, _, half=half):
                 at = pl.ds(pl.multiple_of(i * step, step), step)
-                y = frecv[j, at].astype(F32)
-                is_re, shared = is_re_of(step), shared_of(step)
-                if j == 0:
-                    y = jnp.where(shared, jnp.where(is_re, swap(y) if half else y, 0.0), y)
+                y = source[at].astype(F32)
+                is_re = is_re_of(step)
+                if shares:
+                    y = jnp.where(shared_of(step), jnp.where(is_re, swap(y) if half else y, 0.0), y)
                 other = swap(y)
                 ops[half, 0, at] = y.astype(BF16)
                 ops[half, 1, at] = jnp.where(is_re, other, -other).astype(BF16)
@@ -163,25 +176,45 @@
 
             lax.fori_loop(0, steps, operands, 0)
         for half in range(2):
-            use = half if j == 0 else 0
-
-            def columns(i, _, use=use, j=j):
+            use = half if shares else 0
+
+            def columns(i, _, use=use):
                 at = pl.ds(pl.multiple_of(i * step, step), step)
-                spec[j, at] = (mm(cos[at], ops[use, 0]) + mm(sin[at], ops[use, 1])).astype(BF16)
+                target[at] = (mm(cos[at], ops[use, 0]) + mm(sin[at], ops[use, 1])).astype(BF16)
                 return 0
 
             lax.fori_loop(half * steps // 2, (half + 1) * steps // 2, columns, 0)
-        if j == 0:
-            middle = height // 2
+        if shares:
             rows = lax.broadcasted_iota(jnp.int32, (16, LANES), 0)
             mark = (rows == 0) & shared_of(16) & ~is_re_of(16)
             top = swap(mm(cos[middle : middle + 16], ops[0, 0]))
             bottom = swap(mm(cos[0:16], ops[1, 0]))
-            spec[0, 0:16] = jnp.where(mark, top, spec[0, 0:16].astype(F32)).astype(BF16)
-            spec[0, middle : middle + 16] = jnp.where(
-                mark, bottom, spec[0, middle : middle + 16].astype(F32)
+            target[0:16] = jnp.where(mark, top, target[0:16].astype(F32)).astype(BF16)
+            target[middle : middle + 16] = jnp.where(
+                mark, bottom, target[middle : middle + 16].astype(F32)
             ).astype(BF16)
-        partner_copy(j).start()
+
+    rows_to_columns(0)
+    pl.semaphore_wait(barrier, 2 * n - 1)
+    for k in order:
+        forward_copy(0, k).start()
+    for k in range(n):
+        far_copy(k).start()
+    for j in range(chunks):
+        if j + 1 < chunks:
+            rows_to_columns(j + 1)
+        for k in range(1, n):
+            forward_copy(j, k).wait_recv()
+        if j + 1 < chunks:
+            for k in order:
+                forward_copy(j + 1, k).start()
+        if j == 0:
+            loads[3].wait()
+            loads[4].wait()
+        transform(frecv.at[j], spec.at[j], j == 0)
+        if j == 1:
+            for half in range(2):
+                partner_copy(j, half).start()
 
     def gather(j):
         for k in range(1, n):
@@ -202,9 +235,22 @@
                 if j == chunks - 1:
                     value = value * scale
                 out[p, :, c : c + 256] = value
+            if j == chunks - 1:
+                store(p).start()
 
     for j in range(chunks):
-        partner_copy(j).wait_recv()
+        if j == 0:
+            for k in range(n):
+                far_copy(k).wait_recv()
+        else:
+            partner_copy(j, 0).wait_recv()
+            if j < chunks - 1:
+                partner_copy(j, 1).wait_recv()
+        if j + 2 < chunks:
+            for half in range(2):
+                partner_copy(j + 2, half).start()
+        if j == 0:
+            transform(far, pspec.at[0], True)
 
         def cross(i, _, j=j, bottom=False):
             at = pl.ds(pl.multiple_of(i * step, step), step)
@@ -214,9 +260,9 @@
             far = pspec[j, at].astype(F32)
             own_turned = pltpu.roll(own, block, 1)
             far_turned = pltpu.roll(far, block, 1)
-            want_left = jnp.where(slot_low, pairs[0], 1 - pairs[2])
-            want_right = jnp.where(slot_low, lax.rem(pairs[1], 2), 1 - lax.rem(pairs[3], 2))
-            want_far = jnp.where(slot_low, pairs[1], pairs[3]) >= 2
+            want_left = jnp.where(slot_low, pairs[0, 0, 0], 1 - pairs[0, 1, 0])
+            want_right = jnp.where(slot_low, lax.rem(pairs[0, 0, 1], 2), 1 - lax.rem(pairs[0, 1, 1], 2))
+            want_far = jnp.where(slot_low, pairs[0, 0, 1], pairs[0, 1, 1]) >= 2
             left = jnp.where(want_left == 0, own, own_turned)
             right = jnp.where(
                 want_right == 0, jnp.where(want_far, far, own), jnp.where(want_far, far_turned, own_turned)
@@ -254,9 +300,18 @@
             return 0
 
         lax.fori_loop(0, steps // 2, functools.partial(cross, bottom=False), 0)
+        split = 0 < j == chunks - 1
+        if split:
+
+            def part(i, _):
+                at = pl.ds(pl.multiple_of(i * step, step), step)
+                zsum[at] = mm(cos[at, 0:middle], ops[0, 0, 0:middle]) + mm(sin[at, 0:middle], ops[0, 1, 0:middle])
+                return 0
+
+            lax.fori_loop(0, steps, part, 0)
+            partner_copy(j, 1).wait_recv()
         lax.fori_loop(steps // 2, steps, functools.partial(cross, bottom=True), 0)
         if j == 0:
-            middle = height // 2
             rows = lax.broadcasted_iota(jnp.int32, (16, LANES), 0)
             mark = (rows == 0) & shared_of(16)
             is_re = is_re_of(16)
@@ -264,18 +319,19 @@
             ops[0, 0, middle : middle + 16] = jnp.where(
                 mark & is_re, swap(qfix[0]), ops[0, 0, middle : middle + 16].astype(F32)
             ).astype(BF16)
-
-        def inverse(i, _, j=j):
-            at = pl.ds(pl.multiple_of(i * step, step), step)
-            zsend[j, at] = (mm(cos[at], ops[0, 0]) + mm(sin[at], ops[0, 1])).astype(BF16)
-            return 0
-
-        lax.fori_loop(0, steps, inverse, 0)
-        for k in range(1, n):
-            back_copy(j, k).start()
-        zrecv[j, me] = zsend[j, pl.ds(pl.multiple_of(me * band, band), band)]
+        for k in order + [0]:
+            at = pl.ds(pl.multiple_of(lax.rem(me + k, n) * band, band), band)
+            if split:
+                z = mm(cos[at, middle:], ops[0, 0, middle:]) + mm(sin[at, middle:], ops[0, 1, middle:]) + zsum[at]
+            else:
+                z = mm(cos[at], ops[0, 0]) + mm(sin[at], ops[0, 1])
+            if k:
+                zsend[j, at] = z.astype(BF16)
+                back_copy(j, k).start()
+            else:
+                zrecv[j, me] = z.astype(BF16)
         if j == 0:
-            loads[4].wait()
+            loads[5].wait()
         else:
             gather(j - 1)
     gather(chunks - 1)
@@ -284,7 +340,13 @@
         for k in range(1, n):
             forward_copy(j, k).wait_send()
             back_copy(j, k).wait_send()
-        partner_copy(j).wait_send()
+        if j > 0:
+            for half in range(2):
+                partner_copy(j, half).wait_send()
+    for k in range(n):
+        far_copy(k).wait_send()
+    for p in range(2):
+        store(p).wait()
 
 
 def local(tiles, pairs, counts):
@@ -297,18 +359,20 @@
     chunks = width // 2 // n // cw
     cos_h, sin_h = dft_tables(height)
     forward, inverse = row_tables(width, n, cw)
-    rows = lax.dynamic_slice(jnp.asarray(hann(height)), (lax.axis_index("rows") * band,), (band,))
+    hann_h = np.repeat(hann(height).reshape(n, band, 1), LANES, axis=2)
     vmem = pl.BlockSpec(memory_space=pltpu.VMEM)
     smem = pl.BlockSpec(memory_space=pltpu.SMEM)
-    hbm = pl.BlockSpec(memory_space=pl.ANY)
+    hbm = pl.BlockSpec(memory_space=pltpu.HBM)
     dma = pltpu.SemaphoreType.DMA
     return pl.pallas_call(
         functools.partial(kernel, n, nb, cw),
         out_shape=jax.ShapeDtypeStruct((slots, band, width), F32),
-        in_specs=[smem, smem, hbm, vmem, vmem, hbm, hbm, hbm, hbm],
-        out_specs=vmem,
+        in_specs=[smem, smem, hbm, hbm, vmem, hbm, hbm, hbm, hbm],
+        out_specs=hbm,
         scratch_shapes=[
+            pltpu.VMEM((slots, band, width), F32),
             pltpu.VMEM(tiles.shape, F32),
+            pltpu.VMEM((band, LANES), F32),
             pltpu.VMEM(forward.shape, BF16),
             pltpu.VMEM((height, height), BF16),
             pltpu.VMEM((height, height), BF16),
@@ -316,28 +380,33 @@
             pltpu.VMEM(tiles.shape, BF16),
             pltpu.VMEM((chunks, n, band, LANES), BF16),
             pltpu.VMEM((chunks, height, LANES), BF16),
+            pltpu.VMEM((height, LANES), BF16),
             pltpu.VMEM((2, 2, height, LANES), BF16),
             pltpu.VMEM((chunks, height, LANES), BF16),
             pltpu.VMEM((chunks, height, LANES), BF16),
             pltpu.VMEM((2, 16, LANES), F32),
+            pltpu.VMEM((height, LANES), F32),
             pltpu.VMEM((chunks, height, LANES), BF16),
             pltpu.VMEM((chunks, n, band, LANES), BF16),
-            dma((5,)),
+            dma((6,)),
+            dma((slots,)),
             dma((chunks, n - 1)),
             dma((chunks, n - 1)),
-            dma((chunks,)),
-            dma((chunks,)),
+            dma((n,)),
+            dma((n,)),
+            dma((chunks, 2)),
+            dma((chunks, 2)),
             dma((chunks, n - 1)),
             dma((chunks, n - 1)),
         ],
         compiler_params=pltpu.CompilerParams(
-            collective_id=0, has_side_effects=True, vmem_limit_bytes=48 * 1024 * 1024
+            collective_id=0, has_side_effects=True, vmem_limit_bytes=56 * 1024 * 1024
         ),
     )(
-        pairs.reshape(-1),
+        pairs,
         counts,
         tiles,
-        rows[:, None],
+        jnp.asarray(hann_h),
         jnp.asarray(hann(width))[None, :],
         jnp.asarray(forward),
         jnp.asarray(cos_h.astype(ml_dtypes.bfloat16)),

time: 75.1 us -> 66.8 us (0.89)
  Pallas kernels: 68.9 us -> 62.8 us
  local copies, waits for them, and re-layouts: 5.25 us -> 3.16 us
    pallas_call x1, Pallas kernels: 68.9 us -> 62.8 us  [local(): pl.pallas_call(functools.partial(kernel, n, nb, cw), out_shape=jax.ShapeD...]
    dynamic_slice x1 -> x0, local copies, waits for them, and re-layouts: 0.77 us -> none  [local(): lax.dynamic_slice(jnp.asarray(hann(height)), (lax.axis_index('rows') * ba...]
    reshape x1 -> x0, local copies, waits for them, and re-layouts: 0.76 us -> none  [local(): pairs.reshape(-1)]
    unnamed x5 -> x1, local copies, waits for them, and re-layouts: 3.6 us -> 3.16 us
where the time goes in v2:
time: 66.8 us; the launch traced here: 66.6 us
  Pallas kernels  62.8 us (94%)
  local copies, waits for them, and re-layouts  3.16 us (5%)
    pallas_call x1, Pallas kernels, local(): pl.pallas_call(functools.partial(kernel, n, nb, cw), out_shape=jax.ShapeD...  62.8 us
    unnamed x1, local copies, waits for them, and re-layouts  3.16 us

profile of v2, /device:TPU:1, one launch (start us, length us, event | category | flops | bytes accessed | tf_op | source)
XLA Modules:
  0.0 66.6 jit_solution(6552443086362632036)
XLA Ops:
  0.7 62.8 %shard_map.91 = f32[2,256,1024]{2,1,0:T(8,128)} custom-call(s32[1,2,2]{2,1,0:T(2,128)} %pairs.1, s32[1]{0:T(128)S(6)} %copy.11.counts, f32[2,256,1024]{2,1,0:T(8,128)} %tiles_hbm.1, f32[4,256,128]{2,1,0:T(8,128)} %constant.12.clone.hann_hbm, f32[1,1024]{1,0:T(1,128)} %constant.21.hann_w, bf16[4,1024,256]{2,1,0:T(8,128)(2,1)} %constant.14.clone.fwd_hbm, ...), custom_call_target="tpu_custom_call" | custom-call | tf_op jit(solution)/shard_map/pallas_call | solution.py:367
  63.5 3.2 %copy.12 = f32[2,256,1024]{2,1,0:T(8,128)} copy(f32[2,256,1024]{2,1,0:T(8,128)} %shard_map.91) | data formatting | bytes 4194304

commit v3 on v2

--- a/solution.py
+++ b/solution.py
@@ -54,9 +54,9 @@
 def kernel(
     n, nb, cw,
     pairs, counts, tiles_hbm, hann_hbm, hann_w, fwd_hbm, cos_hbm, sin_hbm, inv_hbm,
-    out_hbm,
-    out, tiles, hann_h, fwd, cos, sin, inv, shaded, fsend, frecv, far, ops, spec, pspec, qfix, zsum, zsend, zrecv,
-    load_sem, out_sem, fs, fr, gs, gr, zs, zr, bs, br,
+    out,
+    tiles, hann_h, fwd, cos, sin, inv, shaded, fsend, frecv, far, ops, spec, pspec, qfix, zsum, zsend, zrecv,
+    load_sem, fs, fr, gs, gr, zs, zr, bs, br,
 ):
     me = lax.axis_index("rows")
     blk = lax.axis_index("blk")
@@ -64,19 +64,28 @@
     groups, band, width = tiles.shape
     height = cos.shape[0]
     chunks = spec.shape[0]
-    step = min(256, height // 2)
+    step = min(256, height // 4)
     steps = height // step
     block = LANES // 2
     middle = height // 2
+    parts = zs.shape[1]
     order = [n // 2] + [k for k in range(1, n) if k != n // 2]
 
     loads = [
         pltpu.make_async_copy(src, dst, load_sem.at[i])
         for i, (src, dst) in enumerate(
-            [(tiles_hbm, tiles), (hann_hbm.at[me], hann_h), (fwd_hbm, fwd), (cos_hbm, cos), (sin_hbm, sin), (inv_hbm, inv)]
+            [
+                (tiles_hbm, tiles),
+                (hann_hbm.at[me], hann_h),
+                (fwd_hbm.at[0], fwd.at[0]),
+                (fwd_hbm.at[pl.ds(1, chunks - 1)], fwd.at[pl.ds(1, chunks - 1)]),
+                (cos_hbm, cos),
+                (sin_hbm, sin),
+                (inv_hbm, inv),
+            ]
         )
     ]
-    for load in loads:
+    for load in loads[:3]:
         load.start()
 
     barrier = pltpu.get_barrier_semaphore()
@@ -119,19 +128,16 @@
             device_id_type=MESH,
         )
 
-    def partner_copy(j, half):
-        at = pl.ds(half * middle, middle)
+    def partner_copy(j, part):
+        at = pl.ds(part * (height // parts), height // parts)
         return pltpu.make_async_remote_copy(
             src_ref=spec.at[j, at],
             dst_ref=pspec.at[j, at],
-            send_sem=zs.at[j, half],
-            recv_sem=zr.at[j, half],
+            send_sem=zs.at[j, part],
+            recv_sem=zr.at[j, part],
             device_id={"blk": partner},
             device_id_type=MESH,
         )
-
-    def store(p):
-        return pltpu.make_async_copy(out.at[p], out_hbm.at[p], out_sem.at[p])
 
     def back_copy(j, k):
         return pltpu.make_async_remote_copy(
@@ -148,6 +154,8 @@
     for g in range(groups):
         shaded[g] = (tiles[g] * (hann_h[:, 0:1] * hann_w[...])).astype(BF16)
     loads[2].wait()
+    for load in loads[3:6]:
+        load.start()
     low = lanes_of(band) < block
 
     def rows_to_columns(j):
@@ -196,37 +204,42 @@
 
     rows_to_columns(0)
     pl.semaphore_wait(barrier, 2 * n - 1)
-    for k in order:
-        forward_copy(0, k).start()
     for k in range(n):
         far_copy(k).start()
-    for j in range(chunks):
-        if j + 1 < chunks:
-            rows_to_columns(j + 1)
+    loads[3].wait()
+    turns = [1, 0] + list(range(2, chunks))
+    rows_to_columns(turns[0])
+    for k in order:
+        forward_copy(turns[0], k).start()
+    for at, j in enumerate(turns):
+        later = turns[at + 1] if at + 1 < chunks else None
+        if later:
+            rows_to_columns(later)
         for k in range(1, n):
             forward_copy(j, k).wait_recv()
-        if j + 1 < chunks:
+        if later is not None:
             for k in order:
-                forward_copy(j + 1, k).start()
-        if j == 0:
-            loads[3].wait()
+                forward_copy(later, k).start()
+        if at == 0:
             loads[4].wait()
+            loads[5].wait()
+            loads[6].start()
         transform(frecv.at[j], spec.at[j], j == 0)
         if j == 1:
-            for half in range(2):
-                partner_copy(j, half).start()
+            for part in range(parts):
+                partner_copy(j, part).start()
 
     def gather(j):
         for k in range(1, n):
             back_copy(j, k).wait_recv()
-        parts = [[], []]
+        slabs = [[], []]
         for m in range(n // 2):
             a = zrecv[j, 2 * m].astype(F32)
             b = zrecv[j, 2 * m + 1].astype(F32)
-            parts[0].append(jnp.where(low, a, pltpu.roll(b, block, 1)).astype(BF16))
-            parts[1].append(jnp.where(low, pltpu.roll(a, block, 1), b).astype(BF16))
+            slabs[0].append(jnp.where(low, a, pltpu.roll(b, block, 1)).astype(BF16))
+            slabs[1].append(jnp.where(low, pltpu.roll(a, block, 1), b).astype(BF16))
         for p in range(2):
-            z = jnp.concatenate(parts[p], axis=1)
+            z = jnp.concatenate(slabs[p], axis=1)
             scale = jnp.where(p < counts[0], 1.0, 0.0).astype(F32)
             for c in range(0, width, 256):
                 value = mm(z, inv[j, :, c : c + 256])
@@ -235,20 +248,17 @@
                 if j == chunks - 1:
                     value = value * scale
                 out[p, :, c : c + 256] = value
-            if j == chunks - 1:
-                store(p).start()
 
     for j in range(chunks):
         if j == 0:
             for k in range(n):
                 far_copy(k).wait_recv()
         else:
-            partner_copy(j, 0).wait_recv()
-            if j < chunks - 1:
-                partner_copy(j, 1).wait_recv()
+            for part in range(parts if j < chunks - 1 else 1):
+                partner_copy(j, part).wait_recv()
         if j + 2 < chunks:
-            for half in range(2):
-                partner_copy(j + 2, half).start()
+            for part in range(parts):
+                partner_copy(j + 2, part).start()
         if j == 0:
             transform(far, pspec.at[0], True)
 
@@ -299,18 +309,29 @@
             ops[0, 1, at] = for_sin.astype(BF16)
             return 0
 
-        lax.fori_loop(0, steps // 2, functools.partial(cross, bottom=False), 0)
         split = 0 < j == chunks - 1
+        done = 0
         if split:
-
-            def part(i, _):
-                at = pl.ds(pl.multiple_of(i * step, step), step)
-                zsum[at] = mm(cos[at, 0:middle], ops[0, 0, 0:middle]) + mm(sin[at, 0:middle], ops[0, 1, 0:middle])
-                return 0
-
-            lax.fori_loop(0, steps, part, 0)
-            partner_copy(j, 1).wait_recv()
-        lax.fori_loop(steps // 2, steps, functools.partial(cross, bottom=True), 0)
+            for part in range(parts):
+                if part:
+                    partner_copy(j, part).wait_recv()
+                first, last = part * steps // parts, (part + 1) * steps // parts
+                lax.fori_loop(first, last, cross, 0)
+                if part == parts - 1:
+                    break
+                done = (part + 1) * height // parts
+
+                def share(i, _, since=part * height // parts, until=done):
+                    at = pl.ds(pl.multiple_of(i * step, step), step)
+                    z = mm(cos[at, since:until], ops[0, 0, since:until])
+                    z = z + mm(sin[at, since:until], ops[0, 1, since:until])
+                    zsum[at] = z + zsum[at] if since else z
+                    return 0
+
+                lax.fori_loop(0, steps, share, 0)
+        else:
+            lax.fori_loop(0, steps // 2, cross, 0)
+            lax.fori_loop(steps // 2, steps, functools.partial(cross, bottom=True), 0)
         if j == 0:
             rows = lax.broadcasted_iota(jnp.int32, (16, LANES), 0)
             mark = (rows == 0) & shared_of(16)
@@ -322,7 +343,7 @@
         for k in order + [0]:
             at = pl.ds(pl.multiple_of(lax.rem(me + k, n) * band, band), band)
             if split:
-                z = mm(cos[at, middle:], ops[0, 0, middle:]) + mm(sin[at, middle:], ops[0, 1, middle:]) + zsum[at]
+                z = mm(cos[at, done:], ops[0, 0, done:]) + mm(sin[at, done:], ops[0, 1, done:]) + zsum[at]
             else:
                 z = mm(cos[at], ops[0, 0]) + mm(sin[at], ops[0, 1])
             if k:
@@ -331,7 +352,7 @@
             else:
                 zrecv[j, me] = z.astype(BF16)
         if j == 0:
-            loads[5].wait()
+            loads[6].wait()
         else:
             gather(j - 1)
     gather(chunks - 1)
@@ -341,12 +362,10 @@
             forward_copy(j, k).wait_send()
             back_copy(j, k).wait_send()
         if j > 0:
-            for half in range(2):
-                partner_copy(j, half).wait_send()
+            for part in range(parts):
+                partner_copy(j, part).wait_send()
     for k in range(n):
         far_copy(k).wait_send()
-    for p in range(2):
-        store(p).wait()
 
 
 def local(tiles, pairs, counts):
@@ -368,9 +387,8 @@
         functools.partial(kernel, n, nb, cw),
         out_shape=jax.ShapeDtypeStruct((slots, band, width), F32),
         in_specs=[smem, smem, hbm, hbm, vmem, hbm, hbm, hbm, hbm],
-        out_specs=hbm,
+        out_specs=vmem,
         scratch_shapes=[
-            pltpu.VMEM((slots, band, width), F32),
             pltpu.VMEM(tiles.shape, F32),
             pltpu.VMEM((band, LANES), F32),
             pltpu.VMEM(forward.shape, BF16),
@@ -388,19 +406,18 @@
             pltpu.VMEM((height, LANES), F32),
             pltpu.VMEM((chunks, height, LANES), BF16),
             pltpu.VMEM((chunks, n, band, LANES), BF16),
-            dma((6,)),
-            dma((slots,)),
+            dma((7,)),
             dma((chunks, n - 1)),
             dma((chunks, n - 1)),
             dma((n,)),
             dma((n,)),
-            dma((chunks, 2)),
-            dma((chunks, 2)),
+            dma((chunks, 4)),
+            dma((chunks, 4)),
             dma((chunks, n - 1)),
             dma((chunks, n - 1)),
         ],
         compiler_params=pltpu.CompilerParams(
-            collective_id=0, has_side_effects=True, vmem_limit_bytes=56 * 1024 * 1024
+            collective_id=0, has_side_effects=True, vmem_limit_bytes=51 * 1024 * 1024
         ),
     )(
         pairs,

time: 66.8 us -> 68.6 us (1.027)
  Pallas kernels: 62.8 us -> 63.9 us
    pallas_call x1, Pallas kernels: 62.8 us -> 63.9 us  [local(): pl.pallas_call(functools.partial(kernel, n, nb, cw), out_shape=jax.ShapeD...]
    unnamed x1 -> x7, local copies, waits for them, and re-layouts: 3.16 us -> 3.72 us
where the time goes in v3:
time: 68.6 us; the launch traced here: 68.3 us
  Pallas kernels  63.9 us (93%)
  local copies, waits for them, and re-layouts  3.72 us (5%)
    pallas_call x1, Pallas kernels, local(): pl.pallas_call(functools.partial(kernel, n, nb, cw), out_shape=jax.ShapeD...  63.9 us
    unnamed x7, local copies, waits for them, and re-layouts  3.72 us

profile of v3, /device:TPU:1, one launch (start us, length us, event | category | flops | bytes accessed | tf_op | source)
XLA Modules:
  0.0 68.3 jit_solution(14046326656096364340)
XLA Ops:
  0.7 0.0 copy-start
  0.7 1.0 %copy-done = f32[4,256,128]{2,1,0:T(8,128)S(1)} copy-done((f32[4,256,128]{2,1,0:T(8,128)S(1)}, f32[4,256,128]{2,1,0:T(8,128)}, u32[]{:S(2)}) %copy-start) | copy-done | bytes 524312
  1.7 0.0 copy-start.1
  1.7 0.7 %copy-done.1 = f32[1,1024]{1,0:T(1,128)S(1)} copy-done((f32[1,1024]{1,0:T(1,128)S(1)}, f32[1,1024]{1,0:T(1,128)}, u32[]{:S(2)}) %copy-start.1) | copy-done | bytes 4120
  2.4 0.0 copy-start.2
  2.4 0.7 copy-done.2
  3.1 63.9 %shard_map.91 = f32[2,256,1024]{2,1,0:T(8,128)S(1)} custom-call(s32[1,2,2]{2,1,0:T(2,128)S(1)} %copy-done.2, s32[1]{0:T(128)S(6)} %copy.11.counts, f32[2,256,1024]{2,1,0:T(8,128)} %tiles_hbm.1, f32[4,256,128]{2,1,0:T(8,128)S(1)} %copy-done, f32[1,1024]{1,0:T(1,128)S(1)} %copy-done.1, bf16[4,1024,256]{2,1,0:T(8,128)(2,1)} %constant.14.clone.fwd_hbm, ...), custom_call_target="tpu_custom_call" | custom-call | tf_op jit(solution)/shard_map/pallas_call | solution.py:386
  67.0 1.3 %copy.12 = f32[2,256,1024]{2,1,0:T(8,128)} copy(f32[2,256,1024]{2,1,0:T(8,128)S(1)} %shard_map.91) | data formatting | bytes 4194304
Async XLA Ops:
  0.7 1.0 %copy-start = (f32[4,256,128]{2,1,0:T(8,128)S(1)}, f32[4,256,128]{2,1,0:T(8,128)}, u32[]{:S(2)}) copy-start(f32[4,256,128]{2,1,0:T(8,128)} %constant.12.clone.hann_hbm) | copy-start | bytes 1572868
  1.7 0.7 %copy-start.1 = (f32[1,1024]{1,0:T(1,128)S(1)}, f32[1,1024]{1,0:T(1,128)}, u32[]{:S(2)}) copy-start(f32[1,1024]{1,0:T(1,128)} %constant.21.hann_w) | copy-start | bytes 12292
  2.4 0.7 copy-start.2

commit v4 on v3

--- a/solution.py
+++ b/solution.py
@@ -53,10 +53,10 @@
 
 def kernel(
     n, nb, cw,
-    pairs, counts, tiles_hbm, hann_hbm, hann_w, fwd_hbm, cos_hbm, sin_hbm, inv_hbm,
+    pairs, counts, tiles_hbm, window_hbm, fwd_hbm, cos_hbm, sin_hbm, inv_hbm,
     out,
-    tiles, hann_h, fwd, cos, sin, inv, shaded, fsend, frecv, far, ops, spec, pspec, qfix, zsum, zsend, zrecv,
-    load_sem, fs, fr, gs, gr, zs, zr, bs, br,
+    tiles, window, fwd, cos, sin, inv, shaded, fsend, frecv, far, ops, spec, pspec, qfix, zsend, zrecv, want, want_far_side,
+    load_sem, fs, fr, gs, gr, zs, zr, bs, br, rs, rr, ws, wr,
 ):
     me = lax.axis_index("rows")
     blk = lax.axis_index("blk")
@@ -69,6 +69,15 @@
     block = LANES // 2
     middle = height // 2
     parts = zs.shape[1]
+    trade = chunks == 4
+    given, kept = chunks - 2, chunks - 1
+    role = blk // (nb // 2)
+
+    def chunk_at(place):
+        if trade and place >= given:
+            return chunks - 1 - role if place == given else chunks - 2 + role
+        return place
+
     order = [n // 2] + [k for k in range(1, n) if k != n // 2]
 
     loads = [
@@ -76,7 +85,7 @@
         for i, (src, dst) in enumerate(
             [
                 (tiles_hbm, tiles),
-                (hann_hbm.at[me], hann_h),
+                (window_hbm.at[me], window),
                 (fwd_hbm.at[0], fwd.at[0]),
                 (fwd_hbm.at[pl.ds(1, chunks - 1)], fwd.at[pl.ds(1, chunks - 1)]),
                 (cos_hbm, cos),
@@ -128,11 +137,31 @@
             device_id_type=MESH,
         )
 
+    def want_copy():
+        return pltpu.make_async_remote_copy(
+            src_ref=want,
+            dst_ref=want_far_side,
+            send_sem=ws.at[0],
+            recv_sem=wr.at[0],
+            device_id={"blk": partner},
+            device_id_type=MESH,
+        )
+
+    def result_copy(k):
+        return pltpu.make_async_remote_copy(
+            src_ref=zsend.at[given, pl.ds(pl.multiple_of(lax.rem(me + k, n) * band, band), band)],
+            dst_ref=zrecv.at[given, me],
+            send_sem=rs.at[k],
+            recv_sem=rr.at[k],
+            device_id={"blk": partner, "rows": lax.rem(me + k, n)},
+            device_id_type=MESH,
+        )
+
     def partner_copy(j, part):
         at = pl.ds(part * (height // parts), height // parts)
         return pltpu.make_async_remote_copy(
             src_ref=spec.at[j, at],
-            dst_ref=pspec.at[j, at],
+            dst_ref=pspec.at[kept if trade and j == given else j, at],
             send_sem=zs.at[j, part],
             recv_sem=zr.at[j, part],
             device_id={"blk": partner},
@@ -152,15 +181,15 @@
     loads[0].wait()
     loads[1].wait()
     for g in range(groups):
-        shaded[g] = (tiles[g] * (hann_h[:, 0:1] * hann_w[...])).astype(BF16)
+        shaded[g] = (tiles[g] * window[...]).astype(BF16)
     loads[2].wait()
     for load in loads[3:6]:
         load.start()
     low = lanes_of(band) < block
 
     def rows_to_columns(j):
-        first = mm(shaded[0], fwd[j])
-        second = mm(shaded[1], fwd[j])
+        first = mm(shaded[0], fwd[chunk_at(j)])
+        second = mm(shaded[1], fwd[chunk_at(j)])
         for m in range(n // 2):
             a = first[:, m * LANES : (m + 1) * LANES]
             b = second[:, m * LANES : (m + 1) * LANES]
@@ -206,8 +235,19 @@
     pl.semaphore_wait(barrier, 2 * n - 1)
     for k in range(n):
         far_copy(k).start()
+    if trade:
+        lanes = lanes_of(8)
+        rows = lax.broadcasted_iota(jnp.int32, (8, LANES), 0)
+        slot_low = lanes < block
+        left_at = jnp.where(slot_low, pairs[0, 0, 0], 1 - pairs[0, 1, 0])
+        right_at = jnp.where(slot_low, lax.rem(pairs[0, 0, 1], 2), 1 - lax.rem(pairs[0, 1, 1], 2))
+        other_side = jnp.where(jnp.where(slot_low, pairs[0, 0, 1], pairs[0, 1, 1]) >= 2, 1, 0)
+        picked = jnp.where(rows == 0, left_at, jnp.where(rows == 1, right_at, other_side))
+        want[...] = picked.astype(F32)
+        want_copy().start()
     loads[3].wait()
-    turns = [1, 0] + list(range(2, chunks))
+    middles = [1] if trade else list(range(1, chunks))
+    turns = [given, 1, kept, 0] if trade else middles[:1] + [0] + middles[1:]
     rows_to_columns(turns[0])
     for k in order:
         forward_copy(turns[0], k).start()
@@ -225,13 +265,16 @@
             loads[5].wait()
             loads[6].start()
         transform(frecv.at[j], spec.at[j], j == 0)
-        if j == 1:
+        if j == given if trade else j > 0:
             for part in range(parts):
                 partner_copy(j, part).start()
 
-    def gather(j):
+    def gather(j, first, last):
         for k in range(1, n):
             back_copy(j, k).wait_recv()
+        add_up(j, first, last)
+
+    def add_up(j, first, last):
         slabs = [[], []]
         for m in range(n // 2):
             a = zrecv[j, 2 * m].astype(F32)
@@ -242,48 +285,39 @@
             z = jnp.concatenate(slabs[p], axis=1)
             scale = jnp.where(p < counts[0], 1.0, 0.0).astype(F32)
             for c in range(0, width, 256):
-                value = mm(z, inv[j, :, c : c + 256])
-                if j > 0:
+                value = mm(z, inv[chunk_at(j), :, c : c + 256])
+                if not first:
                     value = out[p, :, c : c + 256] + value
-                if j == chunks - 1:
+                if last:
                     value = value * scale
                 out[p, :, c : c + 256] = value
 
-    for j in range(chunks):
-        if j == 0:
-            for k in range(n):
-                far_copy(k).wait_recv()
-        else:
-            for part in range(parts if j < chunks - 1 else 1):
-                partner_copy(j, part).wait_recv()
-        if j + 2 < chunks:
-            for part in range(parts):
-                partner_copy(j + 2, part).start()
-        if j == 0:
-            transform(far, pspec.at[0], True)
-
-        def cross(i, _, j=j, bottom=False):
+    def whiten(own_ref, far_ref, picks, shares):
+        def cross(i, _, bottom=False):
             at = pl.ds(pl.multiple_of(i * step, step), step)
             is_re = is_re_of(step)
-            slot_low = lanes_of(step) < block
-            own = spec[j, at].astype(F32)
-            far = pspec[j, at].astype(F32)
+            own = own_ref[at].astype(F32)
+            far = far_ref[at].astype(F32)
             own_turned = pltpu.roll(own, block, 1)
             far_turned = pltpu.roll(far, block, 1)
-            want_left = jnp.where(slot_low, pairs[0, 0, 0], 1 - pairs[0, 1, 0])
-            want_right = jnp.where(slot_low, lax.rem(pairs[0, 0, 1], 2), 1 - lax.rem(pairs[0, 1, 1], 2))
-            want_far = jnp.where(slot_low, pairs[0, 0, 1], pairs[0, 1, 1]) >= 2
-            left = jnp.where(want_left == 0, own, own_turned)
-            right = jnp.where(
-                want_right == 0, jnp.where(want_far, far, own), jnp.where(want_far, far_turned, own_turned)
-            )
+            if picks is None:
+                slot_low = lanes_of(step) < block
+                want_left = jnp.where(slot_low, pairs[0, 0, 0], 1 - pairs[0, 1, 0]) == 0
+                want_right = jnp.where(slot_low, lax.rem(pairs[0, 0, 1], 2), 1 - lax.rem(pairs[0, 1, 1], 2)) == 0
+                want_far = jnp.where(slot_low, pairs[0, 0, 1], pairs[0, 1, 1]) >= 2
+            else:
+                want_left = jnp.broadcast_to(picks[0:1], (step, LANES)) < 0.5
+                want_right = jnp.broadcast_to(picks[1:2], (step, LANES)) < 0.5
+                want_far = jnp.broadcast_to(picks[2:3], (step, LANES)) > 0.5
+            left = jnp.where(want_left, own, own_turned)
+            right = jnp.where(want_right, jnp.where(want_far, far, own), jnp.where(want_far, far_turned, own_turned))
             left_other, right_other = swap(left), swap(right)
             crossed = jnp.where(
                 is_re, left * right + left_other * right_other, left * right_other - left_other * right
             )
             crossed_other = swap(crossed)
             power = crossed * crossed + crossed_other * crossed_other
-            if j == 0:
+            if shares:
                 shared = shared_of(step)
                 rows = lax.broadcasted_iota(jnp.int32, (step, LANES), 0) + i * step
                 single = shared & (lax.rem(rows, height // 2) == 0)
@@ -292,7 +326,7 @@
             q = (crossed / (jnp.sqrt(power) + FLOOR)).astype(BF16).astype(F32)
             other = swap(q)
             for_cos, for_sin = q, jnp.where(is_re, -other, other)
-            if j == 0:
+            if shares:
                 weight = jnp.where(single, 1.0, 2.0)
                 if bottom:
                     for_cos = jnp.where(shared, jnp.where(is_re, 0.0, weight * other), for_cos)
@@ -309,30 +343,9 @@
             ops[0, 1, at] = for_sin.astype(BF16)
             return 0
 
-        split = 0 < j == chunks - 1
-        done = 0
-        if split:
-            for part in range(parts):
-                if part:
-                    partner_copy(j, part).wait_recv()
-                first, last = part * steps // parts, (part + 1) * steps // parts
-                lax.fori_loop(first, last, cross, 0)
-                if part == parts - 1:
-                    break
-                done = (part + 1) * height // parts
-
-                def share(i, _, since=part * height // parts, until=done):
-                    at = pl.ds(pl.multiple_of(i * step, step), step)
-                    z = mm(cos[at, since:until], ops[0, 0, since:until])
-                    z = z + mm(sin[at, since:until], ops[0, 1, since:until])
-                    zsum[at] = z + zsum[at] if since else z
-                    return 0
-
-                lax.fori_loop(0, steps, share, 0)
-        else:
-            lax.fori_loop(0, steps // 2, cross, 0)
-            lax.fori_loop(steps // 2, steps, functools.partial(cross, bottom=True), 0)
-        if j == 0:
+        lax.fori_loop(0, steps // 2, cross, 0)
+        lax.fori_loop(steps // 2, steps, functools.partial(cross, bottom=True), 0)
+        if shares:
             rows = lax.broadcasted_iota(jnp.int32, (16, LANES), 0)
             mark = (rows == 0) & shared_of(16)
             is_re = is_re_of(16)
@@ -340,32 +353,72 @@
             ops[0, 0, middle : middle + 16] = jnp.where(
                 mark & is_re, swap(qfix[0]), ops[0, 0, middle : middle + 16].astype(F32)
             ).astype(BF16)
+
+    def band_of(k):
+        at = pl.ds(pl.multiple_of(lax.rem(me + k, n) * band, band), band)
+        return at, (mm(cos[at], ops[0, 0]) + mm(sin[at], ops[0, 1])).astype(BF16)
+
+    def own_slots(j):
+        whiten(spec.at[j], pspec.at[j], None, j == 0)
         for k in order + [0]:
-            at = pl.ds(pl.multiple_of(lax.rem(me + k, n) * band, band), band)
-            if split:
-                z = mm(cos[at, done:], ops[0, 0, done:]) + mm(sin[at, done:], ops[0, 1, done:]) + zsum[at]
-            else:
-                z = mm(cos[at], ops[0, 0]) + mm(sin[at], ops[0, 1])
+            at, z = band_of(k)
             if k:
-                zsend[j, at] = z.astype(BF16)
+                zsend[j, at] = z
                 back_copy(j, k).start()
             else:
-                zrecv[j, me] = z.astype(BF16)
-        if j == 0:
-            loads[6].wait()
-        else:
-            gather(j - 1)
-    gather(chunks - 1)
+                zrecv[j, me] = z
+
+    for k in range(n):
+        far_copy(k).wait_recv()
+    transform(far, pspec.at[0], True)
+    own_slots(0)
+    loads[6].wait()
+    if trade:
+        partner_copy(1, 0).start()
+        for part in range(parts):
+            partner_copy(given, part).wait_recv()
+        for part in range(1, parts):
+            partner_copy(1, part).start()
+        want_copy().wait_recv()
+        whiten(pspec.at[kept], spec.at[kept], want_far_side, False)
+        for k in range(n):
+            at, z = band_of(k)
+            zsend[given, at] = z
+        own_slots(kept)
+        gather(0, True, False)
+        result_copy(0).start()
+        for part in range(parts):
+            partner_copy(1, part).wait_recv()
+        for k in range(1, n):
+            result_copy(k).start()
+        own_slots(1)
+        gather(kept, False, False)
+        gather(1, False, False)
+        for k in range(n):
+            result_copy(k).wait_recv()
+        add_up(given, False, True)
+    else:
+        for j in middles:
+            for part in range(parts):
+                partner_copy(j, part).wait_recv()
+            own_slots(j)
+            gather(j - 1, j == 1, False)
+        gather(chunks - 1, False, True)
 
     for j in range(chunks):
         for k in range(1, n):
             forward_copy(j, k).wait_send()
-            back_copy(j, k).wait_send()
-        if j > 0:
+            if not (trade and j == given):
+                back_copy(j, k).wait_send()
+        if 0 < j and not (trade and j == kept):
             for part in range(parts):
                 partner_copy(j, part).wait_send()
     for k in range(n):
         far_copy(k).wait_send()
+        if trade:
+            result_copy(k).wait_send()
+    if trade:
+        want_copy().wait_send()
 
 
 def local(tiles, pairs, counts):
@@ -378,7 +431,7 @@
     chunks = width // 2 // n // cw
     cos_h, sin_h = dft_tables(height)
     forward, inverse = row_tables(width, n, cw)
-    hann_h = np.repeat(hann(height).reshape(n, band, 1), LANES, axis=2)
+    window = (hann(height)[:, None] * hann(width)[None, :]).reshape(n, band, width)
     vmem = pl.BlockSpec(memory_space=pltpu.VMEM)
     smem = pl.BlockSpec(memory_space=pltpu.SMEM)
     hbm = pl.BlockSpec(memory_space=pltpu.HBM)
@@ -386,11 +439,11 @@
     return pl.pallas_call(
         functools.partial(kernel, n, nb, cw),
         out_shape=jax.ShapeDtypeStruct((slots, band, width), F32),
-        in_specs=[smem, smem, hbm, hbm, vmem, hbm, hbm, hbm, hbm],
+        in_specs=[smem, smem, hbm, hbm, hbm, hbm, hbm, hbm],
         out_specs=vmem,
         scratch_shapes=[
             pltpu.VMEM(tiles.shape, F32),
-            pltpu.VMEM((band, LANES), F32),
+            pltpu.VMEM((band, width), F32),
             pltpu.VMEM(forward.shape, BF16),
             pltpu.VMEM((height, height), BF16),
             pltpu.VMEM((height, height), BF16),
@@ -403,9 +456,10 @@
             pltpu.VMEM((chunks, height, LANES), BF16),
             pltpu.VMEM((chunks, height, LANES), BF16),
             pltpu.VMEM((2, 16, LANES), F32),
-            pltpu.VMEM((height, LANES), F32),
             pltpu.VMEM((chunks, height, LANES), BF16),
             pltpu.VMEM((chunks, n, band, LANES), BF16),
+            pltpu.VMEM((8, LANES), F32),
+            pltpu.VMEM((8, LANES), F32),
             dma((7,)),
             dma((chunks, n - 1)),
             dma((chunks, n - 1)),
@@ -415,6 +469,10 @@
             dma((chunks, 4)),
             dma((chunks, n - 1)),
             dma((chunks, n - 1)),
+            dma((n,)),
+            dma((n,)),
+            dma((1,)),
+            dma((1,)),
         ],
         compiler_params=pltpu.CompilerParams(
             collective_id=0, has_side_effects=True, vmem_limit_bytes=51 * 1024 * 1024
@@ -423,8 +481,7 @@
         pairs,
         counts,
         tiles,
-        jnp.asarray(hann_h),
-        jnp.asarray(hann(width))[None, :],
+        jnp.asarray(window),
         jnp.asarray(forward),
         jnp.asarray(cos_h.astype(ml_dtypes.bfloat16)),
         jnp.asarray(sin_h.astype(ml_dtypes.bfloat16)),

time: 68.6 us -> 67.5 us (0.984)
  local copies, waits for them, and re-layouts: 3.72 us -> 1.99 us
  Pallas kernels: 63.9 us -> 64.7 us
    unnamed x7 -> x3, local copies, waits for them, and re-layouts: 3.72 us -> 1.99 us
    pallas_call x1, Pallas kernels: 63.9 us -> 64.7 us  [local(): pl.pallas_call(functools.partial(kernel, n, nb, cw), out_shape=jax.ShapeD...]
where the time goes in v4:
time: 67.5 us; the launch traced here: 67.4 us
  Pallas kernels  64.7 us (96%)
  local copies, waits for them, and re-layouts  1.99 us (3%)
    pallas_call x1, Pallas kernels, local(): pl.pallas_call(functools.partial(kernel, n, nb, cw), out_shape=jax.ShapeD...  64.7 us
    unnamed x3, local copies, waits for them, and re-layouts  1.99 us

profile of v4, /device:TPU:1, one launch (start us, length us, event | category | flops | bytes accessed | tf_op | source)
XLA Modules:
  0.0 67.4 jit_solution(11428947322252492437)
XLA Ops:
  0.7 0.0 copy-start
  0.7 0.7 copy-done
  1.3 64.7 %shard_map.82 = f32[2,256,1024]{2,1,0:T(8,128)S(1)} custom-call(s32[1,2,2]{2,1,0:T(2,128)S(1)} %copy-done, s32[1]{0:T(128)S(6)} %copy.10.counts, f32[2,256,1024]{2,1,0:T(8,128)} %tiles_hbm.1, f32[4,256,1024]{2,1,0:T(8,128)} %constant.10.clone.window_hbm, bf16[4,1024,256]{2,1,0:T(8,128)(2,1)} %constant.11.clone.fwd_hbm, ...), custom_call_target="tpu_custom_call" | custom-call | tf_op jit(solution)/shard_map/pallas_call | solution.py:439
  66.1 1.3 %copy.11 = f32[2,256,1024]{2,1,0:T(8,128)} copy(f32[2,256,1024]{2,1,0:T(8,128)S(1)} %shard_map.82) | data formatting | bytes 4194304
Async XLA Ops:
  0.7 0.7 %copy-start = (s32[1,2,2]{2,1,0:T(2,128)S(1)}, s32[1,2,2]{2,1,0:T(2,128)}, u32[]{:S(2)}) copy-start(s32[1,2,2]{2,1,0:T(2,128)} %pairs.1) | copy-start | bytes 52

commit v5 on v4

--- a/solution.py
+++ b/solution.py
@@ -86,8 +86,7 @@
             [
                 (tiles_hbm, tiles),
                 (window_hbm.at[me], window),
-                (fwd_hbm.at[0], fwd.at[0]),
-                (fwd_hbm.at[pl.ds(1, chunks - 1)], fwd.at[pl.ds(1, chunks - 1)]),
+                (fwd_hbm, fwd),
                 (cos_hbm, cos),
                 (sin_hbm, sin),
                 (inv_hbm, inv),
@@ -183,7 +182,7 @@
     for g in range(groups):
         shaded[g] = (tiles[g] * window[...]).astype(BF16)
     loads[2].wait()
-    for load in loads[3:6]:
+    for load in loads[3:]:
         load.start()
     low = lanes_of(band) < block
 
@@ -231,8 +230,13 @@
                 mark, bottom, target[middle : middle + 16].astype(F32)
             ).astype(BF16)
 
+    middles = [1] if trade else list(range(1, chunks))
+    turns = [given, 1, kept, 0] if trade else middles[:1] + [0] + middles[1:]
+    rows_to_columns(turns[0])
+    pl.semaphore_wait(barrier, 2 * n - 1)
+    for k in order:
+        forward_copy(turns[0], k).start()
     rows_to_columns(0)
-    pl.semaphore_wait(barrier, 2 * n - 1)
     for k in range(n):
         far_copy(k).start()
     if trade:
@@ -245,12 +249,6 @@
         picked = jnp.where(rows == 0, left_at, jnp.where(rows == 1, right_at, other_side))
         want[...] = picked.astype(F32)
         want_copy().start()
-    loads[3].wait()
-    middles = [1] if trade else list(range(1, chunks))
-    turns = [given, 1, kept, 0] if trade else middles[:1] + [0] + middles[1:]
-    rows_to_columns(turns[0])
-    for k in order:
-        forward_copy(turns[0], k).start()
     for at, j in enumerate(turns):
         later = turns[at + 1] if at + 1 < chunks else None
         if later:
@@ -261,9 +259,8 @@
             for k in order:
                 forward_copy(later, k).start()
         if at == 0:
+            loads[3].wait()
             loads[4].wait()
-            loads[5].wait()
-            loads[6].start()
         transform(frecv.at[j], spec.at[j], j == 0)
         if j == given if trade else j > 0:
             for part in range(parts):
@@ -372,24 +369,24 @@
         far_copy(k).wait_recv()
     transform(far, pspec.at[0], True)
     own_slots(0)
-    loads[6].wait()
+    loads[5].wait()
     if trade:
-        partner_copy(1, 0).start()
+        for part in range(parts):
+            partner_copy(1, part).start()
         for part in range(parts):
             partner_copy(given, part).wait_recv()
-        for part in range(1, parts):
-            partner_copy(1, part).start()
         want_copy().wait_recv()
         whiten(pspec.at[kept], spec.at[kept], want_far_side, False)
         for k in range(n):
             at, z = band_of(k)
             zsend[given, at] = z
+        for k in range(n // 2):
+            result_copy(k).start()
         own_slots(kept)
         gather(0, True, False)
-        result_copy(0).start()
         for part in range(parts):
             partner_copy(1, part).wait_recv()
-        for k in range(1, n):
+        for k in range(n // 2, n):
             result_copy(k).start()
         own_slots(1)
         gather(kept, False, False)
@@ -460,7 +457,7 @@
             pltpu.VMEM((chunks, n, band, LANES), BF16),
             pltpu.VMEM((8, LANES), F32),
             pltpu.VMEM((8, LANES), F32),
-            dma((7,)),
+            dma((6,)),
             dma((chunks, n - 1)),
             dma((chunks, n - 1)),
             dma((n,)),

time: 67.5 us -> 66 us (0.978)
  Pallas kernels: 64.7 us -> 63.1 us
    pallas_call x1, Pallas kernels: 64.7 us -> 63.1 us  [local(): pl.pallas_call(functools.partial(kernel, n, nb, cw), out_shape=jax.ShapeD...]
where the time goes in v5:
time: 66 us; the launch traced here: 65.8 us
  Pallas kernels  63.1 us (96%)
  local copies, waits for them, and re-layouts  1.99 us (3%)
  between operations  0.67 us (1%)
    pallas_call x1, Pallas kernels, local(): pl.pallas_call(functools.partial(kernel, n, nb, cw), out_shape=jax.ShapeD...  63.1 us
    unnamed x3, local copies, waits for them, and re-layouts  1.99 us

profile of v5, /device:TPU:1, one launch (start us, length us, event | category | flops | bytes accessed | tf_op | source)
XLA Modules:
  0.0 65.8 jit_solution(5017234505388317508)
XLA Ops:
  0.7 0.0 copy-start
  0.7 0.7 %copy-done = s32[1,2,2]{2,1,0:T(2,128)S(1)} copy-done((s32[1,2,2]{2,1,0:T(2,128)S(1)}, s32[1,2,2]{2,1,0:T(2,128)}, u32[]{:S(2)}) %copy-start) | copy-done | bytes 40
  1.3 63.1 %shard_map.82 = f32[2,256,1024]{2,1,0:T(8,128)S(1)} custom-call(s32[1,2,2]{2,1,0:T(2,128)S(1)} %copy-done, s32[1]{0:T(128)S(6)} %copy.10.counts, f32[2,256,1024]{2,1,0:T(8,128)} %tiles_hbm.1, f32[4,256,1024]{2,1,0:T(8,128)} %constant.10.clone.window_hbm, bf16[4,1024,256]{2,1,0:T(8,128)(2,1)} %constant.11.clone.fwd_hbm, ...), custom_call_target="tpu_custom_call" | custom-call | tf_op jit(solution)/shard_map/pallas_call | solution.py:436
  64.5 1.3 %copy.11 = f32[2,256,1024]{2,1,0:T(8,128)} copy(f32[2,256,1024]{2,1,0:T(8,128)S(1)} %shard_map.82) | data formatting | bytes 4194304
Async XLA Ops:
  0.7 0.7 %copy-start = (s32[1,2,2]{2,1,0:T(2,128)S(1)}, s32[1,2,2]{2,1,0:T(2,128)}, u32[]{:S(2)}) copy-start(s32[1,2,2]{2,1,0:T(2,128)} %pairs.1) | copy-start | bytes 52

commit v6 on v5

--- a/solution.py
+++ b/solution.py
@@ -180,15 +180,15 @@
     loads[0].wait()
     loads[1].wait()
     for g in range(groups):
-        shaded[g] = (tiles[g] * window[...]).astype(BF16)
+        shaded[g * band : (g + 1) * band] = (tiles[g] * window[...]).astype(BF16)
     loads[2].wait()
     for load in loads[3:]:
         load.start()
     low = lanes_of(band) < block
 
     def rows_to_columns(j):
-        first = mm(shaded[0], fwd[chunk_at(j)])
-        second = mm(shaded[1], fwd[chunk_at(j)])
+        both = mm(shaded[...], fwd[chunk_at(j)])
+        first, second = both[:band], both[band:]
         for m in range(n // 2):
             a = first[:, m * LANES : (m + 1) * LANES]
             b = second[:, m * LANES : (m + 1) * LANES]
@@ -211,15 +211,9 @@
                 return 0
 
             lax.fori_loop(0, steps, operands, 0)
-        for half in range(2):
-            use = half if shares else 0
-
-            def columns(i, _, use=use):
-                at = pl.ds(pl.multiple_of(i * step, step), step)
-                target[at] = (mm(cos[at], ops[use, 0]) + mm(sin[at], ops[use, 1])).astype(BF16)
-                return 0
-
-            lax.fori_loop(half * steps // 2, (half + 1) * steps // 2, columns, 0)
+        for half in range(2 if shares else 1):
+            first, last = (half * middle, (half + 1) * middle) if shares else (0, height)
+            target[first:last] = (mm(cos[first:last], ops[half, 0]) + mm(sin[first:last], ops[half, 1])).astype(BF16)
         if shares:
             rows = lax.broadcasted_iota(jnp.int32, (16, LANES), 0)
             mark = (rows == 0) & shared_of(16) & ~is_re_of(16)
@@ -278,15 +272,15 @@
             b = zrecv[j, 2 * m + 1].astype(F32)
             slabs[0].append(jnp.where(low, a, pltpu.roll(b, block, 1)).astype(BF16))
             slabs[1].append(jnp.where(low, pltpu.roll(a, block, 1), b).astype(BF16))
-        for p in range(2):
-            z = jnp.concatenate(slabs[p], axis=1)
-            scale = jnp.where(p < counts[0], 1.0, 0.0).astype(F32)
-            for c in range(0, width, 256):
-                value = mm(z, inv[chunk_at(j), :, c : c + 256])
+        z = jnp.concatenate([jnp.concatenate(slab, axis=1) for slab in slabs], axis=0)
+        for c in range(0, width, 256):
+            both = mm(z, inv[chunk_at(j), :, c : c + 256])
+            for p in range(2):
+                value = both[p * band : (p + 1) * band]
                 if not first:
                     value = out[p, :, c : c + 256] + value
                 if last:
-                    value = value * scale
+                    value = value * jnp.where(p < counts[0], 1.0, 0.0).astype(F32)
                 out[p, :, c : c + 256] = value
 
     def whiten(own_ref, far_ref, picks, shares):
@@ -351,19 +345,15 @@
                 mark & is_re, swap(qfix[0]), ops[0, 0, middle : middle + 16].astype(F32)
             ).astype(BF16)
 
-    def band_of(k):
-        at = pl.ds(pl.multiple_of(lax.rem(me + k, n) * band, band), band)
-        return at, (mm(cos[at], ops[0, 0]) + mm(sin[at], ops[0, 1])).astype(BF16)
+    def invert(j):
+        zsend[j] = (mm(cos[...], ops[0, 0]) + mm(sin[...], ops[0, 1])).astype(BF16)
 
     def own_slots(j):
         whiten(spec.at[j], pspec.at[j], None, j == 0)
-        for k in order + [0]:
-            at, z = band_of(k)
-            if k:
-                zsend[j, at] = z
-                back_copy(j, k).start()
-            else:
-                zrecv[j, me] = z
+        invert(j)
+        for k in order:
+            back_copy(j, k).start()
+        zrecv[j, me] = zsend[j, pl.ds(pl.multiple_of(me * band, band), band)]
 
     for k in range(n):
         far_copy(k).wait_recv()
@@ -377,9 +367,7 @@
             partner_copy(given, part).wait_recv()
         want_copy().wait_recv()
         whiten(pspec.at[kept], spec.at[kept], want_far_side, False)
-        for k in range(n):
-            at, z = band_of(k)
-            zsend[given, at] = z
+        invert(given)
         for k in range(n // 2):
             result_copy(k).start()
         own_slots(kept)
@@ -445,7 +433,7 @@
             pltpu.VMEM((height, height), BF16),
             pltpu.VMEM((height, height), BF16),
             pltpu.VMEM(inverse.shape, BF16),
-            pltpu.VMEM(tiles.shape, BF16),
+            pltpu.VMEM((groups * band, width), BF16),
             pltpu.VMEM((chunks, n, band, LANES), BF16),
             pltpu.VMEM((chunks, height, LANES), BF16),
             pltpu.VMEM((height, LANES), BF16),

time: 66 us -> 68.6 us (1.039)
  Pallas kernels: 63.1 us -> 65.8 us
    pallas_call x1, Pallas kernels: 63.1 us -> 65.8 us  [local(): pl.pallas_call(functools.partial(kernel, n, nb, cw), out_shape=jax.ShapeD...]
where the time goes in v6:
time: 68.6 us; the launch traced here: 68.5 us
  Pallas kernels  65.8 us (96%)
  local copies, waits for them, and re-layouts  1.99 us (3%)
    pallas_call x1, Pallas kernels, local(): pl.pallas_call(functools.partial(kernel, n, nb, cw), out_shape=jax.ShapeD...  65.8 us
    unnamed x3, local copies, waits for them, and re-layouts  1.99 us

profile of v6, /device:TPU:1, one launch (start us, length us, event | category | flops | bytes accessed | tf_op | source)
XLA Modules:
  0.0 68.5 jit_solution(17841411697875551796)
XLA Ops:
  0.7 0.0 copy-start
  0.7 0.7 copy-done
  1.3 65.8 %shard_map.82 = f32[2,256,1024]{2,1,0:T(8,128)S(1)} custom-call(s32[1,2,2]{2,1,0:T(2,128)S(1)} %copy-done, s32[1]{0:T(128)S(6)} %copy.10.counts, f32[2,256,1024]{2,1,0:T(8,128)} %tiles_hbm.1, f32[4,256,1024]{2,1,0:T(8,128)} %constant.10.clone.window_hbm, bf16[4,1024,256]{2,1,0:T(8,128)(2,1)} %constant.11.clone.fwd_hbm, ...), custom_call_target="tpu_custom_call" | custom-call | tf_op jit(solution)/shard_map/pallas_call | solution.py:424
  67.1 1.3 %copy.11 = f32[2,256,1024]{2,1,0:T(8,128)} copy(f32[2,256,1024]{2,1,0:T(8,128)S(1)} %shard_map.82) | data formatting | bytes 4194304
Async XLA Ops:
  0.7 0.7 copy-start

commit v7 on v2

--- a/solution.py
+++ b/solution.py
@@ -53,10 +53,10 @@
 
 def kernel(
     n, nb, cw,
-    pairs, counts, tiles_hbm, hann_hbm, hann_w, fwd_hbm, cos_hbm, sin_hbm, inv_hbm,
-    out_hbm,
-    out, tiles, hann_h, fwd, cos, sin, inv, shaded, fsend, frecv, far, ops, spec, pspec, qfix, zsum, zsend, zrecv,
-    load_sem, out_sem, fs, fr, gs, gr, zs, zr, bs, br,
+    pairs, counts, tiles_hbm, window_hbm, fwd_hbm, cos_hbm, sin_hbm, inv_hbm,
+    out,
+    tiles, window, fwd, cos, sin, inv, shaded, fsend, frecv, far, ops, spec, pspec, qfix, zsum, zsend, zrecv,
+    load_sem, fs, fr, gs, gr, zs, zr, bs, br,
 ):
     me = lax.axis_index("rows")
     blk = lax.axis_index("blk")
@@ -73,10 +73,10 @@
     loads = [
         pltpu.make_async_copy(src, dst, load_sem.at[i])
         for i, (src, dst) in enumerate(
-            [(tiles_hbm, tiles), (hann_hbm.at[me], hann_h), (fwd_hbm, fwd), (cos_hbm, cos), (sin_hbm, sin), (inv_hbm, inv)]
+            [(tiles_hbm, tiles), (window_hbm.at[me], window), (fwd_hbm, fwd), (cos_hbm, cos), (sin_hbm, sin), (inv_hbm, inv)]
         )
     ]
-    for load in loads:
+    for load in loads[:3]:
         load.start()
 
     barrier = pltpu.get_barrier_semaphore()
@@ -130,9 +130,6 @@
             device_id_type=MESH,
         )
 
-    def store(p):
-        return pltpu.make_async_copy(out.at[p], out_hbm.at[p], out_sem.at[p])
-
     def back_copy(j, k):
         return pltpu.make_async_remote_copy(
             src_ref=zsend.at[j, pl.ds(pl.multiple_of(lax.rem(me + k, n) * band, band), band)],
@@ -146,8 +143,10 @@
     loads[0].wait()
     loads[1].wait()
     for g in range(groups):
-        shaded[g] = (tiles[g] * (hann_h[:, 0:1] * hann_w[...])).astype(BF16)
+        shaded[g] = (tiles[g] * window[...]).astype(BF16)
     loads[2].wait()
+    for load in loads[3:]:
+        load.start()
     low = lanes_of(band) < block
 
     def rows_to_columns(j):
@@ -235,8 +234,6 @@
                 if j == chunks - 1:
                     value = value * scale
                 out[p, :, c : c + 256] = value
-            if j == chunks - 1:
-                store(p).start()
 
     for j in range(chunks):
         if j == 0:
@@ -345,8 +342,6 @@
                 partner_copy(j, half).wait_send()
     for k in range(n):
         far_copy(k).wait_send()
-    for p in range(2):
-        store(p).wait()
 
 
 def local(tiles, pairs, counts):
@@ -359,7 +354,7 @@
     chunks = width // 2 // n // cw
     cos_h, sin_h = dft_tables(height)
     forward, inverse = row_tables(width, n, cw)
-    hann_h = np.repeat(hann(height).reshape(n, band, 1), LANES, axis=2)
+    window = (hann(height)[:, None] * hann(width)[None, :]).reshape(n, band, width)
     vmem = pl.BlockSpec(memory_space=pltpu.VMEM)
     smem = pl.BlockSpec(memory_space=pltpu.SMEM)
     hbm = pl.BlockSpec(memory_space=pltpu.HBM)
@@ -367,12 +362,11 @@
     return pl.pallas_call(
         functools.partial(kernel, n, nb, cw),
         out_shape=jax.ShapeDtypeStruct((slots, band, width), F32),
-        in_specs=[smem, smem, hbm, hbm, vmem, hbm, hbm, hbm, hbm],
-        out_specs=hbm,
+        in_specs=[smem, smem, hbm, hbm, hbm, hbm, hbm, hbm],
+        out_specs=vmem,
         scratch_shapes=[
-            pltpu.VMEM((slots, band, width), F32),
             pltpu.VMEM(tiles.shape, F32),
-            pltpu.VMEM((band, LANES), F32),
+            pltpu.VMEM((band, width), F32),
             pltpu.VMEM(forward.shape, BF16),
             pltpu.VMEM((height, height), BF16),
             pltpu.VMEM((height, height), BF16),
@@ -389,7 +383,6 @@
             pltpu.VMEM((chunks, height, LANES), BF16),
             pltpu.VMEM((chunks, n, band, LANES), BF16),
             dma((6,)),
-            dma((slots,)),
             dma((chunks, n - 1)),
             dma((chunks, n - 1)),
             dma((n,)),
@@ -400,14 +393,13 @@
             dma((chunks, n - 1)),
         ],
         compiler_params=pltpu.CompilerParams(
-            collective_id=0, has_side_effects=True, vmem_limit_bytes=56 * 1024 * 1024
+            collective_id=0, has_side_effects=True, vmem_limit_bytes=51 * 1024 * 1024
         ),
     )(
         pairs,
         counts,
         tiles,
-        jnp.asarray(hann_h),
-        jnp.asarray(hann(width))[None, :],
+        jnp.asarray(window),
         jnp.asarray(forward),
         jnp.asarray(cos_h.astype(ml_dtypes.bfloat16)),
         jnp.asarray(sin_h.astype(ml_dtypes.bfloat16)),

time: 66.8 us -> 64.8 us (0.970)
  local copies, waits for them, and re-layouts: 3.16 us -> 1.99 us
  Pallas kernels: 62.8 us -> 62 us
    unnamed x1 -> x3, local copies, waits for them, and re-layouts: 3.16 us -> 1.99 us
    pallas_call x1, Pallas kernels: 62.8 us -> 62 us  [local(): pl.pallas_call(functools.partial(kernel, n, nb, cw), out_shape=jax.ShapeD...]
where the time goes in v7:
time: 64.8 us; the launch traced here: 64.7 us
  Pallas kernels  62 us (96%)
  local copies, waits for them, and re-layouts  1.99 us (3%)
  between operations  0.67 us (1%)
    pallas_call x1, Pallas kernels, local(): pl.pallas_call(functools.partial(kernel, n, nb, cw), out_shape=jax.ShapeD...  62 us
    unnamed x3, local copies, waits for them, and re-layouts  1.99 us

profile of v7, /device:TPU:1, one launch (start us, length us, event | category | flops | bytes accessed | tf_op | source)
XLA Modules:
  0.0 64.7 jit_solution(2153687521488137298)
XLA Ops:
  0.7 0.0 copy-start
  0.7 0.7 %copy-done = s32[1,2,2]{2,1,0:T(2,128)S(1)} copy-done((s32[1,2,2]{2,1,0:T(2,128)S(1)}, s32[1,2,2]{2,1,0:T(2,128)}, u32[]{:S(2)}) %copy-start) | copy-done | bytes 40
  1.3 62.0 %shard_map.82 = f32[2,256,1024]{2,1,0:T(8,128)S(1)} custom-call(s32[1,2,2]{2,1,0:T(2,128)S(1)} %copy-done, s32[1]{0:T(128)S(6)} %copy.10.counts, f32[2,256,1024]{2,1,0:T(8,128)} %tiles_hbm.1, f32[4,256,1024]{2,1,0:T(8,128)} %constant.10.clone.window_hbm, bf16[4,1024,256]{2,1,0:T(8,128)(2,1)} %constant.11.clone.fwd_hbm, ...), custom_call_target="tpu_custom_call" | custom-call | tf_op jit(solution)/shard_map/pallas_call | solution.py:362
  63.3 1.3 %copy.11 = f32[2,256,1024]{2,1,0:T(8,128)} copy(f32[2,256,1024]{2,1,0:T(8,128)S(1)} %shard_map.82) | data formatting | bytes 4194304
Async XLA Ops:
  0.7 0.7 %copy-start = (s32[1,2,2]{2,1,0:T(2,128)S(1)}, s32[1,2,2]{2,1,0:T(2,128)}, u32[]{:S(2)}) copy-start(s32[1,2,2]{2,1,0:T(2,128)} %pairs.1) | copy-start | bytes 52
